TPU v7x, 768 devices: a whole 4x8x12 slice. The times are simulated.
768 devices in a mesh: gx: 12 (over z), gy: 64 (over x, y, core).
Axes of the slice: x: 4, y: 8, z: 12, core: 2. Of those that a mesh axis runs over, the one named last changes fastest.
Arguments:
- pressure_now: float32 [384, 2048, 256], P('gx', 'gy'), may hold values from -6 to 6
- pressure_prev: float32 [384, 2048, 256], P('gx', 'gy'), may hold values from -6 to 6
- node_class: int32 [384, 2048, 256], P('gx', 'gy'), may hold values from 0 to 63, as said below
- admittance: float32 [8], replicated, may hold values from 0.05 to 1
Outputs:
- pressure_final: float32 [384, 2048, 256], P('gx', 'gy')
Inputs may be any that keep to these rules, and one draw needn't show every extreme that they name: node_class is 0 for a solid cell; for an air cell it is 8 m + k, with m from 1 to 7 the wall class and k the number of its six neighbours inside the grid whose node_class is not 0. Solid cells come in whole bricks of 32 cells a side and as single cells.
All inputs are finite; a program needn't handle non-finite values.
Results may differ from a plain program's by a relative error of at most 0.00002.
Values sent between devices are 32-bit elements; how exact they have to be, the bound alone decides.
No kernel may reach another device: no remote copies, remote signals or barrier semaphores. Data moves between devices by JAX's collectives and lax.ppermute only.
A program may use at most 128 MiB of HBM per device.

v0:
```python
import jax
import jax.numpy as jnp
from jax import lax
from jax.sharding import PartitionSpec as P

STEPS = 4


THIRD = 1.0 / 3.0
ROOT_THIRD = 0.5773502691896258


def padded_2(cells, sides, width):
    for axis, dim in sides:
        count = lax.axis_size(axis)
        ends = count - 1
        head = lax.slice_in_dim(cells, 0, width, axis=dim)
        tail = lax.slice_in_dim(cells, cells.shape[dim] - width, cells.shape[dim], axis=dim)
        cells = jnp.concatenate(
            [
                lax.ppermute(tail, axis, [(i, (i + 1) % count) for i in range(ends)]),
                cells,
                lax.ppermute(head, axis, [((i + 1) % count, i) for i in range(ends)]),
            ],
            axis=dim,
        )
    return cells


def coefficients(node_class, admittance):
    surface = node_class // 8
    neighbours = (node_class % 8).astype(jnp.float32)
    filled = node_class > 0
    looked = jnp.zeros(node_class.shape, jnp.float32)
    for index in range(admittance.shape[0]):
        looked = jnp.where(surface == index, admittance[index], looked)
    damping = ROOT_THIRD * (6.0 - neighbours) * looked * 0.5
    factor = 1.0 / (1.0 + damping)
    weight_self = jnp.where(filled, (2.0 - neighbours * THIRD) * factor, jnp.float32(0.0))
    weight_side = jnp.where(filled, THIRD * factor, jnp.float32(0.0))
    weight_back = jnp.where(filled, (1.0 - damping) * factor, jnp.float32(0.0))
    return jnp.stack([weight_self, weight_side, weight_back])


def advance_dense(padded, earlier, weights):
    centre = padded[1:-1, 1:-1, 1:-1]
    summed = padded[2:, 1:-1, 1:-1] + padded[:-2, 1:-1, 1:-1]
    summed = summed + padded[1:-1, 2:, 1:-1] + padded[1:-1, :-2, 1:-1]
    summed = summed + padded[1:-1, 1:-1, 2:] + padded[1:-1, 1:-1, :-2]
    return weights[0] * centre + weights[1] * summed - weights[2] * earlier


def advance(padded, earlier, weights):
    return advance_dense(padded, earlier, weights)


def vertical_pad(field):
    return jnp.pad(field, ((0, 0), (0, 0), (1, 1)))


def on_device(pressure_now, pressure_prev, node_class, admittance):
    weights = coefficients(node_class, admittance)
    filled = (node_class > 0).astype(jnp.float32)
    current = pressure_now * filled
    earlier = pressure_prev * filled
    for index in range(STEPS):
        padded = padded_2(current, (("gx", 0), ("gy", 1)), 1)
        following = advance(vertical_pad(padded), earlier, weights)
        earlier = current
        current = following
    return current


def solution(mesh):
    return jax.shard_map(
        on_device,
        mesh=mesh,
        in_specs=(P("gx", "gy", None), P("gx", "gy", None), P("gx", "gy", None), P()),
        out_specs=P("gx", "gy", None),
        check_vma=False,
    )
```

profile of v0, /device:TPU:57, one launch (start us, length us, event | category | flops | bytes accessed | tf_op | source)
XLA Modules:
  0.0 124.1 jit_solution(15483334528876738827)
XLA Ops:
  0.0 0.0 copy-start.3
  0.0 1.7 %broadcast_select_fusion = f32[32,32,256]{2,1,0:T(8,128)S(1)} fusion(f32[32,32,256]{2,1,0:T(8,128)} %param.4, s32[32,32,256]{2,1,0:T(8,128)} %param.6), kind=kLoop, calls=%fused_computation.97 | loop fusion | flops 524288 | bytes 3145728 | tf_op jit(solution)/shard_map/mul | solution.py:64
  1.8 4.0 %collective-permute-start.1 = (f32[1,32,256]{2,1,0:T(8,128)S(1)}, f32[1,32,256]{2,1,0:T(8,128)S(1)}, u32[]{:S(2)}, u32[]{:S(2)}) collective-permute-start(f32[1,32,256]{2,1,0:T(8,128)S(1)} %get-tuple-element.19), channel_id=1, source_target_pairs={{0,64},{64,128},{128,192},{192,256},{256,320},{320,384},{384,448},... | collective-permute-start | bytes 98312 | tf_op jit(solution)/shard_map/ppermute | solution.py:21
  5.8 0.0 copy-start
  5.8 0.0 copy-start.2
  5.8 1.4 %collective-permute-start = (f32[1,32,256]{2,1,0:T(8,128)S(1)}, f32[1,32,256]{2,1,0:T(8,128)S(1)}, u32[]{:S(2)}, u32[]{:S(2)}) collective-permute-start(f32[1,32,256]{2,1,0:T(8,128)S(1)} %get-tuple-element.20), channel_id=1, source_target_pairs={{64,0},{128,64},{192,128},{256,192},{320,256},{384,320},{448,384},... | collective-permute-start | bytes 98312 | tf_op jit(solution)/shard_map/ppermute | solution.py:23
  7.2 0.0 collective-permute-done.1
  7.2 4.0 %collective-permute-done = f32[1,32,256]{2,1,0:T(8,128)S(1)} collective-permute-done((f32[1,32,256]{2,1,0:T(8,128)S(1)}, f32[1,32,256]{2,1,0:T(8,128)S(1)}, u32[]{:S(2)}, u32[]{:S(2)}) %collective-permute-start) | collective-permute-done | bytes 32800 | tf_op jit(solution)/shard_map/ppermute | solution.py:23
  11.2 0.1 pad_maximum_fusion.41
  11.3 4.0 %collective-permute-start.3 = (f32[34,1,256]{2,1,0:T(1,128)S(1)}, f32[34,1,256]{2,1,0:T(1,128)S(1)}, u32[]{:S(2)}, u32[]{:S(2)}) collective-permute-start(f32[34,1,256]{2,1,0:T(1,128)S(1)} %get-tuple-element.11), channel_id=1, source_target_pairs={{0,1},{1,2},{2,3},{3,4},{4,5},{5,6},{6,7},{7,8},{8,9},{9,10},{10,1... | collective-permute-start | bytes 104456 | tf_op jit(solution)/shard_map/ppermute | solution.py:21
  15.3 1.9 %collective-permute-start.2 = (f32[34,1,256]{2,1,0:T(1,128)S(1)}, f32[34,1,256]{2,1,0:T(1,128)S(1)}, u32[]{:S(2)}, u32[]{:S(2)}) collective-permute-start(f32[34,1,256]{2,1,0:T(1,128)S(1)} %get-tuple-element.12), channel_id=1, source_target_pairs={{1,0},{2,1},{3,2},{4,3},{5,4},{6,5},{7,6},{8,7},{9,8},{10,9},{11,1... | collective-permute-start | bytes 104456 | tf_op jit(solution)/shard_map/ppermute | solution.py:23
  17.3 0.0 copy-done.3
  17.3 0.7 fusion.32
  18.0 0.0 collective-permute-done.3
  18.0 4.7 %collective-permute-done.2 = f32[34,1,256]{2,1,0:T(1,128)S(1)} collective-permute-done((f32[34,1,256]{2,1,0:T(1,128)S(1)}, f32[34,1,256]{2,1,0:T(1,128)S(1)}, u32[]{:S(2)}, u32[]{:S(2)}) %collective-permute-start.2) | collective-permute-done | bytes 34848 | tf_op jit(solution)/shard_map/ppermute | solution.py:23
  22.7 0.9 select_maximum_fusion.12
  23.6 0.0 copy-done
  23.6 0.0 copy-done.2
  23.7 8.9 %fusion.22 = f32[32,32,256]{2,1,0:T(8,128)S(1)} fusion(f32[34,34,258]{2,1,0:T(8,128)S(1)} %select_maximum_fusion.12, f32[34,1,256]{2,1,0:T(1,128)S(1)} %collective-permute-done.3, f32[1,32,256]{2,1,0:T(8,128)S(1)} %collective-permute-done, f32[32,32,256]{2,1,0:T(8,128)S(1)} %broadcast_select_fusion, f32[1,32,256]{2,1,0:T(8,128)S(1)} %collective-permute-done.1, ...), kind=kLoop, calls=%fused_computation.76 | loop fusion | flops 18612224 | bytes 6426656 | tf_op jit(solution)/shard_map/sub | solution.py:50
  32.6 4.0 %collective-permute-start.5 = (f32[1,32,256]{2,1,0:T(8,128)S(1)}, f32[1,32,256]{2,1,0:T(8,128)S(1)}, u32[]{:S(2)}, u32[]{:S(2)}) collective-permute-start(f32[1,32,256]{2,1,0:T(8,128)S(1)} %get-tuple-element.17), channel_id=1, source_target_pairs={{0,64},{64,128},{128,192},{192,256},{256,320},{320,384},{384,448},... | collective-permute-start | bytes 98312 | tf_op jit(solution)/shard_map/ppermute | solution.py:21
  36.6 0.0 copy-start.1
  36.6 1.4 %collective-permute-start.4 = (f32[1,32,256]{2,1,0:T(8,128)S(1)}, f32[1,32,256]{2,1,0:T(8,128)S(1)}, u32[]{:S(2)}, u32[]{:S(2)}) collective-permute-start(f32[1,32,256]{2,1,0:T(8,128)S(1)} %get-tuple-element.18), channel_id=1, source_target_pairs={{64,0},{128,64},{192,128},{256,192},{320,256},{384,320},{448,384},... | collective-permute-start | bytes 98312 | tf_op jit(solution)/shard_map/ppermute | solution.py:23
  38.0 0.0 collective-permute-done.5
  38.0 5.2 %collective-permute-done.4 = f32[1,32,256]{2,1,0:T(8,128)S(1)} collective-permute-done((f32[1,32,256]{2,1,0:T(8,128)S(1)}, f32[1,32,256]{2,1,0:T(8,128)S(1)}, u32[]{:S(2)}, u32[]{:S(2)}) %collective-permute-start.4) | collective-permute-done | bytes 32800 | tf_op jit(solution)/shard_map/ppermute | solution.py:23
  43.2 0.1 pad_maximum_fusion.38
  43.3 3.1 %collective-permute-start.7 = (f32[34,1,256]{2,1,0:T(1,128)S(1)}, f32[34,1,256]{2,1,0:T(1,128)S(1)}, u32[]{:S(2)}, u32[]{:S(2)}) collective-permute-start(f32[34,1,256]{2,1,0:T(1,128)S(1)} %get-tuple-element.9), channel_id=1, source_target_pairs={{0,1},{1,2},{2,3},{3,4},{4,5},{5,6},{6,7},{7,8},{8,9},{9,10},{10,1... | collective-permute-start | bytes 104456 | tf_op jit(solution)/shard_map/ppermute | solution.py:21
  46.4 1.9 %collective-permute-start.6 = (f32[34,1,256]{2,1,0:T(1,128)S(1)}, f32[34,1,256]{2,1,0:T(1,128)S(1)}, u32[]{:S(2)}, u32[]{:S(2)}) collective-permute-start(f32[34,1,256]{2,1,0:T(1,128)S(1)} %get-tuple-element.10), channel_id=1, source_target_pairs={{1,0},{2,1},{3,2},{4,3},{5,4},{6,5},{7,6},{8,7},{9,8},{10,9},{11,1... | collective-permute-start | bytes 104456 | tf_op jit(solution)/shard_map/ppermute | solution.py:23
  48.3 0.0 collective-permute-done.7
  48.3 5.4 %collective-permute-done.6 = f32[34,1,256]{2,1,0:T(1,128)S(1)} collective-permute-done((f32[34,1,256]{2,1,0:T(1,128)S(1)}, f32[34,1,256]{2,1,0:T(1,128)S(1)}, u32[]{:S(2)}, u32[]{:S(2)}) %collective-permute-start.6) | collective-permute-done | bytes 34848 | tf_op jit(solution)/shard_map/ppermute | solution.py:23
  53.7 0.9 select_maximum_fusion.8
  54.7 0.0 copy-done.1
  54.7 8.9 %fusion.16 = f32[32,32,256]{2,1,0:T(8,128)S(1)} fusion(f32[34,34,258]{2,1,0:T(8,128)S(1)} %select_maximum_fusion.8, f32[34,1,256]{2,1,0:T(1,128)S(1)} %collective-permute-done.7, f32[1,32,256]{2,1,0:T(8,128)S(1)} %collective-permute-done.4, f32[32,32,256]{2,1,0:T(8,128)S(1)} %fusion.22, f32[1,32,256]{2,1,0:T(8,128)S(1)} %collective-permute-done.5, ...), kind=kLoop, calls=%fused_computation.60 | loop fusion | flops 18612224 | bytes 6426656 | tf_op jit(solution)/shard_map/sub | solution.py:50
  63.6 4.8 %collective-permute-start.9 = (f32[1,32,256]{2,1,0:T(8,128)S(1)}, f32[1,32,256]{2,1,0:T(8,128)S(1)}, u32[]{:S(2)}, u32[]{:S(2)}) collective-permute-start(f32[1,32,256]{2,1,0:T(8,128)S(1)} %get-tuple-element.15), channel_id=1, source_target_pairs={{0,64},{64,128},{128,192},{192,256},{256,320},{320,384},{384,448},... | collective-permute-start | bytes 98312 | tf_op jit(solution)/shard_map/ppermute | solution.py:21
  68.5 1.3 %collective-permute-start.8 = (f32[1,32,256]{2,1,0:T(8,128)S(1)}, f32[1,32,256]{2,1,0:T(8,128)S(1)}, u32[]{:S(2)}, u32[]{:S(2)}) collective-permute-start(f32[1,32,256]{2,1,0:T(8,128)S(1)} %get-tuple-element.16), channel_id=1, source_target_pairs={{64,0},{128,64},{192,128},{256,192},{320,256},{384,320},{448,384},... | collective-permute-start | bytes 98312 | tf_op jit(solution)/shard_map/ppermute | solution.py:23
  69.8 0.0 collective-permute-done.9
  69.8 3.6 %collective-permute-done.8 = f32[1,32,256]{2,1,0:T(8,128)S(1)} collective-permute-done((f32[1,32,256]{2,1,0:T(8,128)S(1)}, f32[1,32,256]{2,1,0:T(8,128)S(1)}, u32[]{:S(2)}, u32[]{:S(2)}) %collective-permute-start.8) | collective-permute-done | bytes 32800 | tf_op jit(solution)/shard_map/ppermute | solution.py:23
  73.4 0.1 pad_maximum_fusion.35
  73.4 3.1 %collective-permute-start.11 = (f32[34,1,256]{2,1,0:T(1,128)S(1)}, f32[34,1,256]{2,1,0:T(1,128)S(1)}, u32[]{:S(2)}, u32[]{:S(2)}) collective-permute-start(f32[34,1,256]{2,1,0:T(1,128)S(1)} %get-tuple-element.7), channel_id=1, source_target_pairs={{0,1},{1,2},{2,3},{3,4},{4,5},{5,6},{6,7},{7,8},{8,9},{9,10},{10,1... | collective-permute-start | bytes 104456 | tf_op jit(solution)/shard_map/ppermute | solution.py:21
  76.5 1.9 %collective-permute-start.10 = (f32[34,1,256]{2,1,0:T(1,128)S(1)}, f32[34,1,256]{2,1,0:T(1,128)S(1)}, u32[]{:S(2)}, u32[]{:S(2)}) collective-permute-start(f32[34,1,256]{2,1,0:T(1,128)S(1)} %get-tuple-element.8), channel_id=1, source_target_pairs={{1,0},{2,1},{3,2},{4,3},{5,4},{6,5},{7,6},{8,7},{9,8},{10,9},{11,1... | collective-permute-start | bytes 104456 | tf_op jit(solution)/shard_map/ppermute | solution.py:23
  78.4 0.0 collective-permute-done.11
  78.5 5.4 %collective-permute-done.10 = f32[34,1,256]{2,1,0:T(1,128)S(1)} collective-permute-done((f32[34,1,256]{2,1,0:T(1,128)S(1)}, f32[34,1,256]{2,1,0:T(1,128)S(1)}, u32[]{:S(2)}, u32[]{:S(2)}) %collective-permute-start.10) | collective-permute-done | bytes 34848 | tf_op jit(solution)/shard_map/ppermute | solution.py:23
  83.9 0.9 select_maximum_fusion.4
  84.8 8.9 %fusion.10 = f32[32,32,256]{2,1,0:T(8,128)S(1)} fusion(f32[34,34,258]{2,1,0:T(8,128)S(1)} %select_maximum_fusion.4, f32[34,1,256]{2,1,0:T(1,128)S(1)} %collective-permute-done.11, f32[1,32,256]{2,1,0:T(8,128)S(1)} %collective-permute-done.8, f32[32,32,256]{2,1,0:T(8,128)S(1)} %fusion.16, f32[1,32,256]{2,1,0:T(8,128)S(1)} %collective-permute-done.9, ...), kind=kLoop, calls=%fused_computation.44 | loop fusion | flops 18350080 | bytes 6426656 | tf_op jit(solution)/shard_map/sub | solution.py:50
  93.7 4.4 %collective-permute-start.13 = (f32[1,32,256]{2,1,0:T(8,128)S(1)}, f32[1,32,256]{2,1,0:T(8,128)S(1)}, u32[]{:S(2)}, u32[]{:S(2)}) collective-permute-start(f32[1,32,256]{2,1,0:T(8,128)S(1)} %get-tuple-element.13), channel_id=1, source_target_pairs={{0,64},{64,128},{128,192},{192,256},{256,320},{320,384},{384,448},... | collective-permute-start | bytes 98312 | tf_op jit(solution)/shard_map/ppermute | solution.py:21
  98.1 1.3 %collective-permute-start.12 = (f32[1,32,256]{2,1,0:T(8,128)S(1)}, f32[1,32,256]{2,1,0:T(8,128)S(1)}, u32[]{:S(2)}, u32[]{:S(2)}) collective-permute-start(f32[1,32,256]{2,1,0:T(8,128)S(1)} %get-tuple-element.14), channel_id=1, source_target_pairs={{64,0},{128,64},{192,128},{256,192},{320,256},{384,320},{448,384},... | collective-permute-start | bytes 98312 | tf_op jit(solution)/shard_map/ppermute | solution.py:23
  99.4 0.0 collective-permute-done.13
  99.4 3.6 %collective-permute-done.12 = f32[1,32,256]{2,1,0:T(8,128)S(1)} collective-permute-done((f32[1,32,256]{2,1,0:T(8,128)S(1)}, f32[1,32,256]{2,1,0:T(8,128)S(1)}, u32[]{:S(2)}, u32[]{:S(2)}) %collective-permute-start.12) | collective-permute-done | bytes 32800 | tf_op jit(solution)/shard_map/ppermute | solution.py:23
  103.0 0.1 pad_maximum_fusion.32
  103.1 3.1 %collective-permute-start.15 = (f32[34,1,256]{2,1,0:T(1,128)S(1)}, f32[34,1,256]{2,1,0:T(1,128)S(1)}, u32[]{:S(2)}, u32[]{:S(2)}) collective-permute-start(f32[34,1,256]{2,1,0:T(1,128)S(1)} %get-tuple-element.5), channel_id=1, source_target_pairs={{0,1},{1,2},{2,3},{3,4},{4,5},{5,6},{6,7},{7,8},{8,9},{9,10},{10,1... | collective-permute-start | bytes 104456 | tf_op jit(solution)/shard_map/ppermute | solution.py:21
  106.1 2.1 %collective-permute-start.14 = (f32[34,1,256]{2,1,0:T(1,128)S(1)}, f32[34,1,256]{2,1,0:T(1,128)S(1)}, u32[]{:S(2)}, u32[]{:S(2)}) collective-permute-start(f32[34,1,256]{2,1,0:T(1,128)S(1)} %get-tuple-element.6), channel_id=1, source_target_pairs={{1,0},{2,1},{3,2},{4,3},{5,4},{6,5},{7,6},{8,7},{9,8},{10,9},{11,1... | collective-permute-start | bytes 104456 | tf_op jit(solution)/shard_map/ppermute | solution.py:23
  108.2 0.0 collective-permute-done.15
  108.2 5.2 %collective-permute-done.14 = f32[34,1,256]{2,1,0:T(1,128)S(1)} collective-permute-done((f32[34,1,256]{2,1,0:T(1,128)S(1)}, f32[34,1,256]{2,1,0:T(1,128)S(1)}, u32[]{:S(2)}, u32[]{:S(2)}) %collective-permute-start.14) | collective-permute-done | bytes 34848 | tf_op jit(solution)/shard_map/ppermute | solution.py:23
  113.5 0.9 select_maximum_fusion
  114.4 9.7 %fusion.4 = f32[32,32,256]{2,1,0:T(8,128)} fusion(f32[34,34,258]{2,1,0:T(8,128)S(1)} %select_maximum_fusion, f32[34,1,256]{2,1,0:T(1,128)S(1)} %collective-permute-done.15, f32[1,32,256]{2,1,0:T(8,128)S(1)} %collective-permute-done.12, f32[32,32,256]{2,1,0:T(8,128)S(1)} %fusion.10, f32[1,32,256]{2,1,0:T(8,128)S(1)} %collective-permute-done.13, ...), kind=kLoop, calls=%fused_computation.28 | loop fusion | flops 18350080 | bytes 6426656 | tf_op jit(solution)/shard_map/sub | solution.py:50
  (4 shorter events, 0.0 us)
Async XLA Ops:
  0.0 17.3 %copy-start.3 = (f32[8]{0:T(128)S(1)}, f32[8]{0:T(128)}, u32[]{:S(2)}) copy-start(f32[8]{0:T(128)} %param.7) | copy-start | bytes 100
  1.8 5.5 %collective-permute-start.1 = (f32[1,32,256]{2,1,0:T(8,128)S(1)}, f32[1,32,256]{2,1,0:T(8,128)S(1)}, u32[]{:S(2)}, u32[]{:S(2)}) collective-permute-start(f32[1,32,256]{2,1,0:T(8,128)S(1)} %get-tuple-element.19), channel_id=1, source_target_pairs={{0,64},{64,128},{128,192},{192,256},{256,320},{320,384},{384,448},... | collective-permute-start | bytes 98312 | tf_op jit(solution)/shard_map/ppermute | solution.py:21
  5.8 17.9 %copy-start = (s32[32,32,256]{2,1,0:T(8,128)S(1)}, s32[32,32,256]{2,1,0:T(8,128)}, u32[]{:S(2)}) copy-start(s32[32,32,256]{2,1,0:T(8,128)} %param.6) | copy-start | bytes 3145732
  5.8 17.9 %copy-start.2 = (f32[32,32,256]{2,1,0:T(8,128)S(1)}, f32[32,32,256]{2,1,0:T(8,128)}, u32[]{:S(2)}) copy-start(f32[32,32,256]{2,1,0:T(8,128)} %param.5) | copy-start | bytes 3145732
  5.8 5.4 %collective-permute-start = (f32[1,32,256]{2,1,0:T(8,128)S(1)}, f32[1,32,256]{2,1,0:T(8,128)S(1)}, u32[]{:S(2)}, u32[]{:S(2)}) collective-permute-start(f32[1,32,256]{2,1,0:T(8,128)S(1)} %get-tuple-element.20), channel_id=1, source_target_pairs={{64,0},{128,64},{192,128},{256,192},{320,256},{384,320},{448,384},... | collective-permute-start | bytes 98312 | tf_op jit(solution)/shard_map/ppermute | solution.py:23
  11.3 6.7 %collective-permute-start.3 = (f32[34,1,256]{2,1,0:T(1,128)S(1)}, f32[34,1,256]{2,1,0:T(1,128)S(1)}, u32[]{:S(2)}, u32[]{:S(2)}) collective-permute-start(f32[34,1,256]{2,1,0:T(1,128)S(1)} %get-tuple-element.11), channel_id=1, source_target_pairs={{0,1},{1,2},{2,3},{3,4},{4,5},{5,6},{6,7},{7,8},{8,9},{9,10},{10,1... | collective-permute-start | bytes 104456 | tf_op jit(solution)/shard_map/ppermute | solution.py:21
  15.3 7.4 %collective-permute-start.2 = (f32[34,1,256]{2,1,0:T(1,128)S(1)}, f32[34,1,256]{2,1,0:T(1,128)S(1)}, u32[]{:S(2)}, u32[]{:S(2)}) collective-permute-start(f32[34,1,256]{2,1,0:T(1,128)S(1)} %get-tuple-element.12), channel_id=1, source_target_pairs={{1,0},{2,1},{3,2},{4,3},{5,4},{6,5},{7,6},{8,7},{9,8},{10,9},{11,1... | collective-permute-start | bytes 104456 | tf_op jit(solution)/shard_map/ppermute | solution.py:23
  32.6 5.5 %collective-permute-start.5 = (f32[1,32,256]{2,1,0:T(8,128)S(1)}, f32[1,32,256]{2,1,0:T(8,128)S(1)}, u32[]{:S(2)}, u32[]{:S(2)}) collective-permute-start(f32[1,32,256]{2,1,0:T(8,128)S(1)} %get-tuple-element.17), channel_id=1, source_target_pairs={{0,64},{64,128},{128,192},{192,256},{256,320},{320,384},{384,448},... | collective-permute-start | bytes 98312 | tf_op jit(solution)/shard_map/ppermute | solution.py:21
  36.6 18.1 %copy-start.1 = (f32[32,32,256]{2,1,0:T(8,128)S(1)}, f32[32,32,256]{2,1,0:T(8,128)}, u32[]{:S(2)}) copy-start(f32[32,32,256]{2,1,0:T(8,128)} %param.4) | copy-start | bytes 3145732
  36.6 6.6 %collective-permute-start.4 = (f32[1,32,256]{2,1,0:T(8,128)S(1)}, f32[1,32,256]{2,1,0:T(8,128)S(1)}, u32[]{:S(2)}, u32[]{:S(2)}) collective-permute-start(f32[1,32,256]{2,1,0:T(8,128)S(1)} %get-tuple-element.18), channel_id=1, source_target_pairs={{64,0},{128,64},{192,128},{256,192},{320,256},{384,320},{448,384},... | collective-permute-start | bytes 98312 | tf_op jit(solution)/shard_map/ppermute | solution.py:23
  43.3 5.0 %collective-permute-start.7 = (f32[34,1,256]{2,1,0:T(1,128)S(1)}, f32[34,1,256]{2,1,0:T(1,128)S(1)}, u32[]{:S(2)}, u32[]{:S(2)}) collective-permute-start(f32[34,1,256]{2,1,0:T(1,128)S(1)} %get-tuple-element.9), channel_id=1, source_target_pairs={{0,1},{1,2},{2,3},{3,4},{4,5},{5,6},{6,7},{7,8},{8,9},{9,10},{10,1... | collective-permute-start | bytes 104456 | tf_op jit(solution)/shard_map/ppermute | solution.py:21
  46.4 7.4 %collective-permute-start.6 = (f32[34,1,256]{2,1,0:T(1,128)S(1)}, f32[34,1,256]{2,1,0:T(1,128)S(1)}, u32[]{:S(2)}, u32[]{:S(2)}) collective-permute-start(f32[34,1,256]{2,1,0:T(1,128)S(1)} %get-tuple-element.10), channel_id=1, source_target_pairs={{1,0},{2,1},{3,2},{4,3},{5,4},{6,5},{7,6},{8,7},{9,8},{10,9},{11,1... | collective-permute-start | bytes 104456 | tf_op jit(solution)/shard_map/ppermute | solution.py:23
  63.6 6.2 %collective-permute-start.9 = (f32[1,32,256]{2,1,0:T(8,128)S(1)}, f32[1,32,256]{2,1,0:T(8,128)S(1)}, u32[]{:S(2)}, u32[]{:S(2)}) collective-permute-start(f32[1,32,256]{2,1,0:T(8,128)S(1)} %get-tuple-element.15), channel_id=1, source_target_pairs={{0,64},{64,128},{128,192},{192,256},{256,320},{320,384},{384,448},... | collective-permute-start | bytes 98312 | tf_op jit(solution)/shard_map/ppermute | solution.py:21
  68.5 4.9 %collective-permute-start.8 = (f32[1,32,256]{2,1,0:T(8,128)S(1)}, f32[1,32,256]{2,1,0:T(8,128)S(1)}, u32[]{:S(2)}, u32[]{:S(2)}) collective-permute-start(f32[1,32,256]{2,1,0:T(8,128)S(1)} %get-tuple-element.16), channel_id=1, source_target_pairs={{64,0},{128,64},{192,128},{256,192},{320,256},{384,320},{448,384},... | collective-permute-start | bytes 98312 | tf_op jit(solution)/shard_map/ppermute | solution.py:23
  73.4 5.0 %collective-permute-start.11 = (f32[34,1,256]{2,1,0:T(1,128)S(1)}, f32[34,1,256]{2,1,0:T(1,128)S(1)}, u32[]{:S(2)}, u32[]{:S(2)}) collective-permute-start(f32[34,1,256]{2,1,0:T(1,128)S(1)} %get-tuple-element.7), channel_id=1, source_target_pairs={{0,1},{1,2},{2,3},{3,4},{4,5},{5,6},{6,7},{7,8},{8,9},{9,10},{10,1... | collective-permute-start | bytes 104456 | tf_op jit(solution)/shard_map/ppermute | solution.py:21
  76.5 7.4 %collective-permute-start.10 = (f32[34,1,256]{2,1,0:T(1,128)S(1)}, f32[34,1,256]{2,1,0:T(1,128)S(1)}, u32[]{:S(2)}, u32[]{:S(2)}) collective-permute-start(f32[34,1,256]{2,1,0:T(1,128)S(1)} %get-tuple-element.8), channel_id=1, source_target_pairs={{1,0},{2,1},{3,2},{4,3},{5,4},{6,5},{7,6},{8,7},{9,8},{10,9},{11,1... | collective-permute-start | bytes 104456 | tf_op jit(solution)/shard_map/ppermute | solution.py:23
  93.7 5.7 %collective-permute-start.13 = (f32[1,32,256]{2,1,0:T(8,128)S(1)}, f32[1,32,256]{2,1,0:T(8,128)S(1)}, u32[]{:S(2)}, u32[]{:S(2)}) collective-permute-start(f32[1,32,256]{2,1,0:T(8,128)S(1)} %get-tuple-element.13), channel_id=1, source_target_pairs={{0,64},{64,128},{128,192},{192,256},{256,320},{320,384},{384,448},... | collective-permute-start | bytes 98312 | tf_op jit(solution)/shard_map/ppermute | solution.py:21
  98.1 4.9 %collective-permute-start.12 = (f32[1,32,256]{2,1,0:T(8,128)S(1)}, f32[1,32,256]{2,1,0:T(8,128)S(1)}, u32[]{:S(2)}, u32[]{:S(2)}) collective-permute-start(f32[1,32,256]{2,1,0:T(8,128)S(1)} %get-tuple-element.14), channel_id=1, source_target_pairs={{64,0},{128,64},{192,128},{256,192},{320,256},{384,320},{448,384},... | collective-permute-start | bytes 98312 | tf_op jit(solution)/shard_map/ppermute | solution.py:23
  103.1 5.2 %collective-permute-start.15 = (f32[34,1,256]{2,1,0:T(1,128)S(1)}, f32[34,1,256]{2,1,0:T(1,128)S(1)}, u32[]{:S(2)}, u32[]{:S(2)}) collective-permute-start(f32[34,1,256]{2,1,0:T(1,128)S(1)} %get-tuple-element.5), channel_id=1, source_target_pairs={{0,1},{1,2},{2,3},{3,4},{4,5},{5,6},{6,7},{7,8},{8,9},{9,10},{10,1... | collective-permute-start | bytes 104456 | tf_op jit(solution)/shard_map/ppermute | solution.py:21
  106.1 7.4 %collective-permute-start.14 = (f32[34,1,256]{2,1,0:T(1,128)S(1)}, f32[34,1,256]{2,1,0:T(1,128)S(1)}, u32[]{:S(2)}, u32[]{:S(2)}) collective-permute-start(f32[34,1,256]{2,1,0:T(1,128)S(1)} %get-tuple-element.6), channel_id=1, source_target_pairs={{1,0},{2,1},{3,2},{4,3},{5,4},{6,5},{7,6},{8,7},{9,8},{10,9},{11,1... | collective-permute-start | bytes 104456 | tf_op jit(solution)/shard_map/ppermute | solution.py:23
where the time goes:
time: 125 us; the launch traced here: 124 us
  starting transfers between devices  43.7 us (35%)
  other arithmetic  42 us (34%)
  waiting for transfers between devices  37.3 us (30%)
    ppermute x8, waiting for transfers between devices, padded_2(): lax.ppermute(head, axis, [((i + 1) % count, i) for i in range(ends)])  37.3 us
    sub x4, other arithmetic, advance_dense(): return weights[0] * centre + weights[1] * summed - weights[2] * earlier  36.3 us
    ppermute x8, starting transfers between devices, padded_2(): lax.ppermute(tail, axis, [(i, (i + 1) % count) for i in range(ends)])  30.4 us
    ppermute x8, starting transfers between devices, padded_2(): lax.ppermute(head, axis, [((i + 1) % count, i) for i in range(ends)])  13.3 us
    concatenate x8, other arithmetic, padded_2(): jnp.concatenate([lax.ppermute(tail, axis, [(i, (i + 1) % count) for i in...  3.95 us
  transfers between devices with their start and end apart: 16, of which 8 were waited for; matrix products, arithmetic and copies ran while one was open for 1% of the time, Pallas kernels for 0%

commit v1 on v0

v1 whole, which is shorter than its diff:
```python
import jax
import jax.numpy as jnp
from jax import lax
from jax.experimental import pallas as pl
from jax.experimental.pallas import tpu as pltpu
from jax.sharding import PartitionSpec as P

STEPS = 4
MATS = 8
TILE = 8
THIRD = 1.0 / 3.0
ROOT_THIRD = 0.5773502691896258
F32 = jnp.float32
VMEM = pl.BlockSpec(memory_space=pltpu.VMEM)
HBM = pl.BlockSpec(memory_space=pl.ANY)
SMEM = pl.BlockSpec(memory_space=pltpu.SMEM)
PARAMS = pltpu.CompilerParams(vmem_limit_bytes=40 * 1024 * 1024)


def cost(flops, moved):
    return pl.CostEstimate(flops=flops, bytes_accessed=moved, transcendentals=0)


def weights(code, table):
    bits = [(code & bit) != 0 for bit in (8, 16, 32)]
    level = [table[index] for index in range(MATS)]
    for bit in bits:
        level = [jnp.where(bit, high, low) for low, high in zip(level[::2], level[1::2])]
    missing = (6 - (code & 7)).astype(F32)
    damping = (ROOT_THIRD * 0.5) * missing * level[0]
    air = code > 0
    side = jnp.where(air, THIRD / (1.0 + damping), 0.0)
    return side, missing, air


def lateral(plane):
    rows, lanes = plane.shape
    lane = lax.broadcasted_iota(jnp.int32, plane.shape, 1)
    below = jnp.where(lane == 0, 0.0, pltpu.roll(plane, 1, 1))
    above = jnp.where(lane == lanes - 1, 0.0, pltpu.roll(plane, lanes - 1, 1))
    return (pltpu.roll(plane, 1, 0) + pltpu.roll(plane, rows - 1, 0)) + (below + above)


def step(plane, across, earlier, side, missing):
    return earlier + side * ((lateral(plane) + across) + (missing * plane - 6.0 * earlier))


def pack_rows(now_ref, prev_ref, class_ref, up_ref, down_ref, edge, code, sems):
    nx, ny, _ = now_ref.shape
    half = nx // 2
    copies = []
    for which, source in enumerate((now_ref, prev_ref, class_ref)):
        for end, start in enumerate((0, ny - TILE)):
            target = code.at[end] if which == 2 else edge.at[which, end]
            copy = pltpu.make_async_copy(
                source.at[:, pl.ds(start, TILE), :], target, sems.at[which, end]
            )
            copy.start()
            copies.append(copy)
    row = lax.broadcasted_iota(jnp.int32, (half, TILE, now_ref.shape[2]), 1)
    lower = row < TILE // 2
    for which in range(3):
        for end in range(2):
            copies[2 * which + end].wait()
            block = code[end].astype(F32) if which == 2 else edge[which, end]
            first, second = block[:half], block[half:]
            place = pl.ds(which * half, half)
            if end:
                up_ref[place] = jnp.where(lower, pltpu.roll(first, TILE // 2, 1), second)
            else:
                down_ref[place] = jnp.where(lower, first, pltpu.roll(second, TILE // 2, 1))


def own_state(table, now_ref, prev_ref, class_ref, c_ref, e_ref, s_ref, m_ref):
    def body(x, carry):
        side, missing, air = weights(class_ref[x], table)
        s_ref[x] = side
        m_ref[x] = missing
        c_ref[x] = jnp.where(air, now_ref[x], 0.0)
        e_ref[x] = jnp.where(air, prev_ref[x], 0.0)
        return carry

    lax.fori_loop(0, class_ref.shape[0], body, 0)


def joined(own, halo, x):
    return jnp.concatenate([own[x], halo[x]], axis=0)


def pack_planes(
    table, low_ref, high_ref, class_ref, c_ref, e_ref, s_ref, m_ref,
    ch_ref, eh_ref, sh_ref, mh_ref, left_ref, right_ref,
):
    nx = c_ref.shape[0]
    half = nx // 2
    row = lax.broadcasted_iota(jnp.int32, (TILE, c_ref.shape[2]), 0)
    lower = row < TILE // 2

    def body(x, carry):
        first, second = [], []
        for which in range(3):
            low, high = low_ref[which * half + x], high_ref[which * half + x]
            first.append(jnp.where(lower, high, pltpu.roll(low, TILE // 2, 0)))
            second.append(jnp.where(lower, pltpu.roll(high, TILE // 2, 0), low))
        for (now, prev, code), place in ((first, x), (second, x + half)):
            side, missing, air = weights(code.astype(jnp.int32), table)
            sh_ref[place] = side
            mh_ref[place] = missing
            ch_ref[place] = jnp.where(air, now, 0.0)
            eh_ref[place] = jnp.where(air, prev, 0.0)
        return carry

    lax.fori_loop(0, half, body, 0)
    own_rows = c_ref.shape[1]
    rows = own_rows + TILE
    for edge, inward, out_ref in ((0, 1, left_ref), (nx - 1, -1, right_ref)):
        place = [edge + inward * depth for depth in range(STEPS)]
        now = [joined(c_ref, ch_ref, x) for x in place]
        prev = [joined(e_ref, eh_ref, x) for x in place[:3]]
        side = [joined(s_ref, sh_ref, x) for x in place[:3]]
        missing = [joined(m_ref, mh_ref, x) for x in place[:3]]
        out_ref[pl.ds(0, rows)] = now[0]
        for taken in range(1, STEPS):
            following = []
            for depth in range(STEPS - taken):
                across = now[depth + 1] if depth == 0 else now[depth - 1] + now[depth + 1]
                following.append(step(now[depth], across, prev[depth], side[depth], missing[depth]))
            prev, now = now, following
            if taken < STEPS - 1:
                out_ref[pl.ds(taken * rows, rows)] = now[0]
            else:
                out_ref[pl.ds(4 * rows, own_rows)] = now[0][:own_rows]
        code = class_ref[place[0]].astype(F32)
        out_ref[pl.ds(3 * rows, own_rows)] = code
        which = 2 * half + (place[0] % half)
        low, high = low_ref[which], high_ref[which]
        if place[0] < half:
            halo = jnp.where(lower, high, pltpu.roll(low, TILE // 2, 0))
        else:
            halo = jnp.where(lower, pltpu.roll(high, TILE // 2, 0), low)
        out_ref[pl.ds(3 * rows + own_rows, TILE)] = halo
        out_ref[pl.ds(4 * rows + own_rows, own_rows)] = class_ref[place[1]].astype(F32)


def evolve(
    c_ref, e_ref, s_ref, m_ref, ch_ref, eh_ref, sh_ref, mh_ref, g_ref, odd, even
):
    nx, own_rows, _ = c_ref.shape
    rows = own_rows + TILE

    def sweep(read, read_earlier, write):
        def body(x, carry):
            before, plane = carry
            after = read(jnp.minimum(x + 1, nx - 1))
            across = before + jnp.where(x == nx - 1, 0.0, after)
            write(
                x,
                step(plane, across, read_earlier(x), joined(s_ref, sh_ref, x), joined(m_ref, mh_ref, x)),
            )
            return plane, after

        first = read(0)
        lax.fori_loop(0, nx, body, (jnp.zeros_like(first), first))

    def store(ref):
        def write(x, value):
            ref[x] = value

        return write

    def last(x, value):
        g_ref[x] = value[:own_rows]

    start = lambda x: joined(c_ref, ch_ref, x)
    sweep(start, lambda x: joined(e_ref, eh_ref, x), store(odd))
    sweep(lambda x: odd[x], start, store(even))
    sweep(lambda x: even[x], lambda x: odd[x], store(odd))
    sweep(lambda x: odd[x], lambda x: even[x], last)


def add_neighbours(
    table, from_left, from_right, left_ref, right_ref, s_ref, m_ref, sh_ref, mh_ref, g_ref, out_ref, edges, sems
):
    nx, own_rows, _ = s_ref.shape
    rows = own_rows + TILE
    inner = pltpu.make_async_copy(
        g_ref.at[pl.ds(STEPS, nx - 2 * STEPS)], out_ref.at[pl.ds(STEPS, nx - 2 * STEPS)], sems.at[0]
    )
    inner.start()
    copies = [inner]
    zeros = jnp.zeros((TILE, s_ref.shape[2]), F32)
    for end, (edge, inward, got, own) in enumerate(
        ((0, 1, from_left, left_ref), (nx - 1, -1, from_right, right_ref))
    ):
        place = [edge + inward * depth for depth in range(STEPS)]
        w0, w1, w2, w3 = [joined(s_ref, sh_ref, x) for x in place]
        k0, k1, k2 = [joined(m_ref, mh_ref, x) for x in place[:3]]
        fm0, fm1, fm2 = [got[pl.ds(t * rows, rows)] for t in range(3)]
        fo0, fo1, fo2 = [own[pl.ds(t * rows, rows)] for t in range(3)]
        fm3 = jnp.concatenate([got[pl.ds(4 * rows, own_rows)], zeros], axis=0)
        v1, j1, _ = weights(got[pl.ds(3 * rows, rows)].astype(jnp.int32), table)
        v2, _, _ = weights(got[pl.ds(4 * rows + own_rows, own_rows)].astype(jnp.int32), table)
        v2 = jnp.concatenate([v2, zeros], axis=0)
        a1 = v1 * fo0
        b1 = w0 * fm0
        a2 = v1 * ((lateral(a1) + j1 * a1) + (b1 + fo1))
        z2 = v2 * a1
        b2 = w0 * ((lateral(b1) + k0 * b1) + (a1 + fm1))
        c2 = w1 * b1
        a3 = a1 + v1 * ((lateral(a2) + j1 * a2) + ((z2 + b2) + (fo2 - 6.0 * a1)))
        b3 = b1 + w0 * ((lateral(b2) + k0 * b2) + ((a2 + c2) + (fm2 - 6.0 * b1)))
        c3 = w1 * ((lateral(c2) + k1 * c2) + b2)
        d3 = w2 * c2
        b4 = b2 + w0 * ((lateral(b3) + k0 * b3) + ((a3 + c3) + (fm3 - 6.0 * b2)))
        c4 = c2 + w1 * ((lateral(c3) + k1 * c3) + ((b3 + d3) - 6.0 * c2))
        d4 = w2 * ((lateral(d3) + k2 * d3) + c3)
        e4 = w3 * d3
        first = min(place)
        for x, value in zip(place, (b4, c4, d4, e4)):
            edges[end, x - first] = g_ref[x] + value[:own_rows]
        copy = pltpu.make_async_copy(edges.at[end], out_ref.at[pl.ds(first, STEPS)], sems.at[end + 1])
        copy.start()
        copies.append(copy)
    for copy in copies:
        copy.wait()


def shifted(array, axis, by):
    ends = lax.axis_size(axis) - 1
    pairs = [(i, i + 1) if by > 0 else (i + 1, i) for i in range(ends)]
    return lax.ppermute(array, axis, pairs)


def vmem(*shape):
    return jax.ShapeDtypeStruct(shape, F32)


def on_device(pressure_now, pressure_prev, node_class, admittance):
    nx, ny, nz = pressure_now.shape
    rows = ny + TILE
    cells = nx * ny * nz
    packed = vmem(3 * nx // 2, TILE, nz)
    up, down = pl.pallas_call(
        pack_rows,
        out_shape=[packed, packed],
        in_specs=[HBM] * 3,
        out_specs=[VMEM] * 2,
        scratch_shapes=[
            pltpu.VMEM((2, 2, nx, TILE, nz), F32),
            pltpu.VMEM((2, nx, TILE, nz), jnp.int32),
            pltpu.SemaphoreType.DMA((3, 2)),
        ],
        compiler_params=PARAMS,
        cost_estimate=cost(cells, 4 * cells),
        name="pack_rows",
    )(pressure_now, pressure_prev, node_class)
    low = shifted(up, "gy", 1)
    high = shifted(down, "gy", -1)
    own = pl.pallas_call(
        own_state,
        out_shape=[vmem(nx, ny, nz)] * 4,
        in_specs=[SMEM] + [VMEM] * 3,
        out_specs=[VMEM] * 4,
        compiler_params=PARAMS,
        cost_estimate=cost(30 * cells, 28 * cells),
        name="own_state",
    )(admittance, pressure_now, pressure_prev, node_class)
    plane = vmem(4 * rows + 2 * ny, nz)
    *halo, left, right = pl.pallas_call(
        pack_planes,
        out_shape=[vmem(nx, TILE, nz)] * 4 + [plane, plane],
        in_specs=[SMEM] + [VMEM] * 7,
        out_specs=[VMEM] * 6,
        compiler_params=PARAMS,
        cost_estimate=cost(10 * cells, 4 * cells),
        name="pack_planes",
    )(admittance, low, high, node_class, *own)
    from_left = shifted(right, "gx", 1)
    from_right = shifted(left, "gx", -1)
    free = pl.pallas_call(
        evolve,
        out_shape=vmem(nx, ny, nz),
        in_specs=[VMEM] * 8,
        out_specs=VMEM,
        scratch_shapes=[pltpu.VMEM((nx, rows, nz), F32)] * 2,
        compiler_params=PARAMS,
        cost_estimate=cost(60 * cells, 40 * cells),
        name="evolve",
    )(*own, *halo)
    return pl.pallas_call(
        add_neighbours,
        out_shape=vmem(nx, ny, nz),
        in_specs=[SMEM] + [VMEM] * 9,
        out_specs=HBM,
        scratch_shapes=[pltpu.VMEM((2, STEPS, ny, nz), F32), pltpu.SemaphoreType.DMA((3,))],
        compiler_params=PARAMS,
        cost_estimate=cost(10 * cells, 4 * cells),
        name="add_neighbours",
    )(admittance, from_left, from_right, left, right, own[2], own[3], halo[2], halo[3], free)


def solution(mesh):
    return jax.shard_map(
        on_device,
        mesh=mesh,
        in_specs=(P("gx", "gy", None), P("gx", "gy", None), P("gx", "gy", None), P()),
        out_specs=P("gx", "gy", None),
        check_vma=False,
    )
```

time: 125 us -> 43 us (0.34)
  the two profiles are of different devices: /device:TPU:57 before, /device:TPU:219 now
where the time goes in v1:
time: 43 us; the launch traced here: 42.7 us
  Pallas kernels  18.1 us (42%)
  starting transfers between devices  14.2 us (33%)
  waiting for transfers between devices  6.66 us (15%)
  local copies, waits for them, and re-layouts  3.69 us (9%)
    ppermute x4, starting transfers between devices, shifted(): return lax.ppermute(array, axis, pairs)  14.2 us
    pallas_call x1, Pallas kernels, on_device(): pl.pallas_call(evolve, out_shape=vmem(nx, ny, nz), in_specs=[VMEM] * 8, o...  12.8 us
    ppermute x4, waiting for transfers between devices, shifted(): return lax.ppermute(array, axis, pairs)  6.66 us
    unnamed x10, local copies, waits for them, and re-layouts  3.69 us
    pallas_call x1, Pallas kernels, on_device(): pl.pallas_call(add_neighbours, out_shape=vmem(nx, ny, nz), in_specs=[SMEM...  1.91 us
    pallas_call x1, Pallas kernels, on_device(): pl.pallas_call(own_state, out_shape=[vmem(nx, ny, nz)] * 4, in_specs=[SME...  1.7 us
    pallas_call x1, Pallas kernels, on_device(): pl.pallas_call(pack_planes, out_shape=[vmem(nx, TILE, nz)] * 4 + [plane,...  1.45 us
  transfers between devices with their start and end apart: 4, of which 2 were waited for; matrix products, arithmetic and copies ran while one was open for 0% of the time, Pallas kernels for 34%

profile of v1, /device:TPU:219, one launch (start us, length us, event | category | flops | bytes accessed | tf_op | source)
XLA Modules:
  0.0 42.7 jit_solution(12203915501027044876)
XLA Ops:
  0.0 0.0 copy-start
  0.0 1.2 %copy-done = s32[32,32,256]{2,1,0:T(8,128)S(1)} copy-done((s32[32,32,256]{2,1,0:T(8,128)S(1)}, s32[32,32,256]{2,1,0:T(8,128)}, u32[]{:S(2)}) %copy-start) | copy-done | bytes 1048600
  1.2 0.0 copy-start.2
  1.2 1.2 %copy-done.2 = f32[32,32,256]{2,1,0:T(8,128)S(1)} copy-done((f32[32,32,256]{2,1,0:T(8,128)S(1)}, f32[32,32,256]{2,1,0:T(8,128)}, u32[]{:S(2)}) %copy-start.2) | copy-done | bytes 1048600
  2.5 0.0 copy-start.3
  2.5 1.2 %copy-done.3 = f32[32,32,256]{2,1,0:T(8,128)S(1)} copy-done((f32[32,32,256]{2,1,0:T(8,128)S(1)}, f32[32,32,256]{2,1,0:T(8,128)}, u32[]{:S(2)}) %copy-start.3) | copy-done | bytes 1048600
  3.7 0.3 pack_rows.1
  4.0 0.0 copy-start.4
  4.0 5.0 %collective-permute-start = (f32[48,8,256]{2,1,0:T(8,128)S(1)}, f32[48,8,256]{2,1,0:T(8,128)S(1)}, u32[]{:S(2)}, u32[]{:S(2)}) collective-permute-start(f32[48,8,256]{2,1,0:T(8,128)S(1)} %get-tuple-element.17), channel_id=1, source_target_pairs={{0,1},{1,2},{2,3},{3,4},{4,5},{5,6},{6,7},{7,8},{8,9},{9,10},{10,1... | collective-permute-start | bytes 1179656 | tf_op jit(solution)/shard_map/ppermute | solution.py:231
  9.0 0.0 copy-start.1
  9.0 2.1 %collective-permute-start.1 = (f32[48,8,256]{2,1,0:T(8,128)S(1)}, f32[48,8,256]{2,1,0:T(8,128)S(1)}, u32[]{:S(2)}, u32[]{:S(2)}) collective-permute-start(f32[48,8,256]{2,1,0:T(8,128)S(1)} %get-tuple-element.18), channel_id=1, source_target_pairs={{1,0},{2,1},{3,2},{4,3},{5,4},{6,5},{7,6},{8,7},{9,8},{10,9},{11,1... | collective-permute-start | bytes 1179656 | tf_op jit(solution)/shard_map/ppermute | solution.py:231
  11.0 0.0 copy-done.4
  11.0 1.7 %own_state.1 = (f32[32,32,256]{2,1,0:T(8,128)S(1)}, f32[32,32,256]{2,1,0:T(8,128)S(1)}, f32[32,32,256]{2,1,0:T(8,128)S(1)}, f32[32,32,256]{2,1,0:T(8,128)S(1)}) custom-call(f32[8]{0:T(128)S(1)} %copy-done.4, f32[32,32,256]{2,1,0:T(8,128)S(1)} %copy-done.2, f32[32,32,256]{2,1,0:T(8,128)S(1)} %copy-done.3, s32[32,32,256]{2,1,0:T(8,128)S(1)} %copy-done), custom_call_target="tpu_custom_call" | custom-call | flops 7864320 | bytes 7340032 | tf_op jit(solution)/shard_map/own_state/pallas_call | solution.py:259
  12.8 0.9 %collective-permute-done.low_ref = f32[48,8,256]{2,1,0:T(8,128)S(1)} collective-permute-done((f32[48,8,256]{2,1,0:T(8,128)S(1)}, f32[48,8,256]{2,1,0:T(8,128)S(1)}, u32[]{:S(2)}, u32[]{:S(2)}) %collective-permute-start) | collective-permute-done | bytes 393248 | tf_op jit(solution)/shard_map/ppermute | solution.py:231
  13.7 5.8 %collective-permute-done.1.high_ref = f32[48,8,256]{2,1,0:T(8,128)S(1)} collective-permute-done((f32[48,8,256]{2,1,0:T(8,128)S(1)}, f32[48,8,256]{2,1,0:T(8,128)S(1)}, u32[]{:S(2)}, u32[]{:S(2)}) %collective-permute-start.1) | collective-permute-done | bytes 393248 | tf_op jit(solution)/shard_map/ppermute | solution.py:231
  19.4 0.0 copy-done.1
  19.4 1.5 %pack_planes.1 = (f32[32,8,256]{2,1,0:T(8,128)S(1)}, f32[32,8,256]{2,1,0:T(8,128)S(1)}, f32[32,8,256]{2,1,0:T(8,128)S(1)}, f32[32,8,256]{2,1,0:T(8,128)S(1)}, f3...) custom-call(f32[8]{0:T(128)S(1)} %copy-done.4, f32[48,8,256]{2,1,0:T(8,128)S(1)} %collective-permute-done.low_ref, ...), custom_call_target="tpu_custom_call" | custom-call | flops 2621440 | bytes 1048576 | tf_op jit(solution)/shard_map/pack_planes/pallas_call | solution.py:269
  20.9 5.2 %collective-permute-start.2 = (f32[224,256]{1,0:T(8,128)S(1)}, f32[224,256]{1,0:T(8,128)S(1)}, u32[]{:S(2)}, u32[]{:S(2)}) collective-permute-start(f32[224,256]{1,0:T(8,128)S(1)} %get-tuple-element.23.right_ref), channel_id=1, source_target_pairs={{0,64},{64,128},{128,192},{192,256},{256,320},{320,384},{384,448},... | collective-permute-start | bytes 688136 | tf_op jit(solution)/shard_map/ppermute | solution.py:231
  26.1 1.9 %collective-permute-start.3 = (f32[224,256]{1,0:T(8,128)S(1)}, f32[224,256]{1,0:T(8,128)S(1)}, u32[]{:S(2)}, u32[]{:S(2)}) collective-permute-start(f32[224,256]{1,0:T(8,128)S(1)} %get-tuple-element.24.left_ref), channel_id=1, source_target_pairs={{64,0},{128,64},{192,128},{256,192},{320,256},{384,320},{448,384},... | collective-permute-start | bytes 688136 | tf_op jit(solution)/shard_map/ppermute | solution.py:231
  28.0 12.8 %evolve.1.g_ref = f32[32,32,256]{2,1,0:T(8,128)S(1)} custom-call(f32[32,32,256]{2,1,0:T(8,128)S(1)} %get-tuple-element.19.c_ref, f32[32,32,256]{2,1,0:T(8,128)S(1)} %get-tuple-element.20.e_ref, f32[32,32,256]{2,1,0:T(8,128)S(1)} %get-tuple-element.21.s_ref, f32[32,32,256]{2,1,0:T(8,128)S(1)} %get-tuple-element.22.m_ref, ...), custom_call_target="tpu_custom_call" | custom-call | flops 15728640 | bytes 10485760 | tf_op jit(solution)/shard_map/evolve/pallas_call | solution.py:280
  40.8 0.0 collective-permute-done.2.from_left
  40.8 0.0 collective-permute-done.3.from_right
  40.8 1.9 %add_neighbours.1 = f32[32,32,256]{2,1,0:T(8,128)} custom-call(f32[8]{0:T(128)S(1)} %copy-done.4, f32[224,256]{1,0:T(8,128)S(1)} %collective-permute-done.2.from_left, f32[224,256]{1,0:T(8,128)S(1)} %collective-permute-done.3.from_right, f32[224,256]{1,0:T(8,128)S(1)} %get-tuple-element.24.left_ref, f32[224,256]{1,0:T(8,128)S(1)} %get-tuple-element.23.right_ref, ...), custom_call_target="tpu_custom_call" | custom-call | flops 2621440 | bytes 1048576 | tf_op jit(solution)/shard_map/add_neighbours/pallas_call | solution.py:290
Async XLA Ops:
  0.0 1.2 %copy-start = (s32[32,32,256]{2,1,0:T(8,128)S(1)}, s32[32,32,256]{2,1,0:T(8,128)}, u32[]{:S(2)}) copy-start(s32[32,32,256]{2,1,0:T(8,128)} %class_ref.5) | copy-start | bytes 3145732
  1.2 1.2 %copy-start.2 = (f32[32,32,256]{2,1,0:T(8,128)S(1)}, f32[32,32,256]{2,1,0:T(8,128)}, u32[]{:S(2)}) copy-start(f32[32,32,256]{2,1,0:T(8,128)} %now_ref.3) | copy-start | bytes 3145732
  2.5 1.2 %copy-start.3 = (f32[32,32,256]{2,1,0:T(8,128)S(1)}, f32[32,32,256]{2,1,0:T(8,128)}, u32[]{:S(2)}) copy-start(f32[32,32,256]{2,1,0:T(8,128)} %prev_ref.3) | copy-start | bytes 3145732
  4.0 7.1 %copy-start.4 = (f32[8]{0:T(128)S(1)}, f32[8]{0:T(128)}, u32[]{:S(2)}) copy-start(f32[8]{0:T(128)} %table.5) | copy-start | bytes 100
  4.0 9.7 %collective-permute-start = (f32[48,8,256]{2,1,0:T(8,128)S(1)}, f32[48,8,256]{2,1,0:T(8,128)S(1)}, u32[]{:S(2)}, u32[]{:S(2)}) collective-permute-start(f32[48,8,256]{2,1,0:T(8,128)S(1)} %get-tuple-element.17), channel_id=1, source_target_pairs={{0,1},{1,2},{2,3},{3,4},{4,5},{5,6},{6,7},{7,8},{8,9},{9,10},{10,1... | collective-permute-start | bytes 1179656 | tf_op jit(solution)/shard_map/ppermute | solution.py:231
  9.0 10.5 %copy-start.1 = (s32[32,32,256]{2,1,0:T(8,128)S(1)}, s32[32,32,256]{2,1,0:T(8,128)}, u32[]{:S(2)}) copy-start(s32[32,32,256]{2,1,0:T(8,128)} %class_ref.5) | copy-start | bytes 3145732
  9.0 10.4 %collective-permute-start.1 = (f32[48,8,256]{2,1,0:T(8,128)S(1)}, f32[48,8,256]{2,1,0:T(8,128)S(1)}, u32[]{:S(2)}, u32[]{:S(2)}) collective-permute-start(f32[48,8,256]{2,1,0:T(8,128)S(1)} %get-tuple-element.18), channel_id=1, source_target_pairs={{1,0},{2,1},{3,2},{4,3},{5,4},{6,5},{7,6},{8,7},{9,8},{10,9},{11,1... | collective-permute-start | bytes 1179656 | tf_op jit(solution)/shard_map/ppermute | solution.py:231
  20.9 19.9 %collective-permute-start.2 = (f32[224,256]{1,0:T(8,128)S(1)}, f32[224,256]{1,0:T(8,128)S(1)}, u32[]{:S(2)}, u32[]{:S(2)}) collective-permute-start(f32[224,256]{1,0:T(8,128)S(1)} %get-tuple-element.23.right_ref), channel_id=1, source_target_pairs={{0,64},{64,128},{128,192},{192,256},{256,320},{320,384},{384,448},... | collective-permute-start | bytes 688136 | tf_op jit(solution)/shard_map/ppermute | solution.py:231
  26.1 14.7 %collective-permute-start.3 = (f32[224,256]{1,0:T(8,128)S(1)}, f32[224,256]{1,0:T(8,128)S(1)}, u32[]{:S(2)}, u32[]{:S(2)}) collective-permute-start(f32[224,256]{1,0:T(8,128)S(1)} %get-tuple-element.24.left_ref), channel_id=1, source_target_pairs={{64,0},{128,64},{192,128},{256,192},{320,256},{384,320},{448,384},... | collective-permute-start | bytes 688136 | tf_op jit(solution)/shard_map/ppermute | solution.py:231

commit v2 on v1

v2 whole, which is shorter than its diff:
```python
import jax
import jax.numpy as jnp
from jax import lax
from jax.experimental import pallas as pl
from jax.experimental.pallas import tpu as pltpu
from jax.sharding import PartitionSpec as P

STEPS = 4
MATS = 8
TILE = 8
LANES = 128
CHUNKS = 4
THIRD = 1.0 / 3.0
ROOT_THIRD = 0.5773502691896258
F32 = jnp.float32
VMEM = pl.BlockSpec(memory_space=pltpu.VMEM)
HBM = pl.BlockSpec(memory_space=pltpu.HBM)
SMEM = pl.BlockSpec(memory_space=pltpu.SMEM)
PARAMS = pltpu.CompilerParams(vmem_limit_bytes=40 * 1024 * 1024)


def cost(flops, moved):
    return pl.CostEstimate(flops=flops, bytes_accessed=moved, transcendentals=0)


def weights(code, table):
    bits = [(code & bit) != 0 for bit in (8, 16, 32)]
    level = [table[index] for index in range(MATS)]
    for bit in bits:
        level = [jnp.where(bit, high, low) for low, high in zip(level[::2], level[1::2])]
    missing = (6 - (code & 7)).astype(F32)
    damping = (ROOT_THIRD * 0.5) * missing * level[0]
    air = code > 0
    side = jnp.where(air, THIRD / (1.0 + damping), 0.0)
    return side, missing, air


def lateral(plane):
    rows, lanes = plane.shape
    tiles = [plane[start : start + TILE] for start in range(0, rows, TILE)]
    row = lax.broadcasted_iota(jnp.int32, tiles[0].shape, 0)
    down = [pltpu.roll(tile, 1, 0) for tile in tiles]
    up = [pltpu.roll(tile, TILE - 1, 0) for tile in tiles]
    along_rows = jnp.concatenate(
        [
            jnp.where(row == 0, down[i - 1], down[i])
            + jnp.where(row == TILE - 1, up[(i + 1) % len(tiles)], up[i])
            for i in range(len(tiles))
        ],
        axis=0,
    )
    parts = [plane[:, start : start + LANES] for start in range(0, lanes, LANES)]
    lane = lax.broadcasted_iota(jnp.int32, parts[0].shape, 1)
    from_below = [0.0] + [pltpu.roll(part, 1, 1) for part in parts]
    from_above = [pltpu.roll(part, LANES - 1, 1) for part in parts] + [0.0]
    along_lanes = jnp.concatenate(
        [
            jnp.where(lane == 0, from_below[i], from_below[i + 1])
            + jnp.where(lane == LANES - 1, from_above[i + 1], from_above[i])
            for i in range(len(parts))
        ],
        axis=1,
    )
    return along_rows + along_lanes


def step(plane, across, earlier, side, missing):
    return earlier + side * ((lateral(plane) + across) + (missing * plane - 6.0 * earlier))


def pack_rows(now_ref, prev_ref, class_ref, cross_ref, chip_ref, edge, code, sems):
    odd = lax.axis_index("gy") % 2 == 1
    nx, ny, _ = now_ref.shape
    half = nx // 2
    copies = []
    for which, source in enumerate((now_ref, prev_ref, class_ref)):
        for end, start in enumerate((0, ny - TILE)):
            target = code.at[end] if which == 2 else edge.at[which, end]
            copy = pltpu.make_async_copy(
                source.at[:, pl.ds(start, TILE), :], target, sems.at[which, end]
            )
            copy.start()
            copies.append(copy)
    row = lax.broadcasted_iota(jnp.int32, (half, TILE, now_ref.shape[2]), 1)
    lower = row < TILE // 2
    for which in range(3):
        blocks = []
        for end in range(2):
            copies[2 * which + end].wait()
            block = code[end].astype(F32) if which == 2 else edge[which, end]
            blocks.append((block[:half], block[half:]))
        (first, second), (first_up, second_up) = blocks
        down = jnp.where(lower, first, pltpu.roll(second, TILE // 2, 1))
        up = jnp.where(lower, pltpu.roll(first_up, TILE // 2, 1), second_up)
        place = pl.ds(which * half, half)
        cross_ref[place] = jnp.where(odd, up, down)
        chip_ref[place] = jnp.where(odd, down, up)


def own_state(
    table, now_hbm, prev_hbm, class_hbm, c_ref, e_ref, s_ref, m_ref, class_ref, now, prev, sems
):
    nx = class_ref.shape[0]
    chunk = nx // CHUNKS
    copies = []
    for index in range(CHUNKS):
        place = pl.ds(index * chunk, chunk)
        for which, (source, target) in enumerate(
            ((class_hbm, class_ref), (now_hbm, now), (prev_hbm, prev))
        ):
            copy = pltpu.make_async_copy(source.at[place], target.at[place], sems.at[which, index])
            copy.start()
            copies.append(copy)

    def body(x, carry):
        side, missing, air = weights(class_ref[x], table)
        s_ref[x] = side
        m_ref[x] = missing
        c_ref[x] = jnp.where(air, now[x], 0.0)
        e_ref[x] = jnp.where(air, prev[x], 0.0)
        return carry

    for index in range(CHUNKS):
        for copy in copies[3 * index : 3 * index + 3]:
            copy.wait()
        lax.fori_loop(index * chunk, (index + 1) * chunk, body, 0, unroll=4)


def joined(own, halo, x):
    return jnp.concatenate([own[x], halo[x]], axis=0)


def pack_planes(
    table, cross_ref, chip_ref, class_ref, c_ref, e_ref, s_ref, m_ref,
    ch_ref, eh_ref, sh_ref, mh_ref, first_ref, second_ref,
):
    nx = c_ref.shape[0]
    odd_y = lax.axis_index("gy") % 2 == 1
    odd_x = lax.axis_index("gx") % 2 == 1

    def received(index):
        cross, chip = cross_ref[index], chip_ref[index]
        return jnp.where(odd_y, chip, cross), jnp.where(odd_y, cross, chip)

    half = nx // 2
    row = lax.broadcasted_iota(jnp.int32, (TILE, c_ref.shape[2]), 0)
    lower = row < TILE // 2

    def body(x, carry):
        first, second = [], []
        for which in range(3):
            low, high = received(which * half + x)
            first.append(jnp.where(lower, high, pltpu.roll(low, TILE // 2, 0)))
            second.append(jnp.where(lower, pltpu.roll(high, TILE // 2, 0), low))
        for (now, prev, code), place in ((first, x), (second, x + half)):
            side, missing, air = weights(code.astype(jnp.int32), table)
            sh_ref[place] = side
            mh_ref[place] = missing
            ch_ref[place] = jnp.where(air, now, 0.0)
            eh_ref[place] = jnp.where(air, prev, 0.0)
        return carry

    lax.fori_loop(0, half, body, 0)
    own_rows = c_ref.shape[1]
    rows = own_rows + TILE
    sides = []
    for edge, inward in ((0, 1), (nx - 1, -1)):
        out = {}
        place = [edge + inward * depth for depth in range(STEPS)]
        now = [joined(c_ref, ch_ref, x) for x in place]
        prev = [joined(e_ref, eh_ref, x) for x in place[:3]]
        side = [joined(s_ref, sh_ref, x) for x in place[:3]]
        missing = [joined(m_ref, mh_ref, x) for x in place[:3]]
        out[0] = now[0]
        for taken in range(1, STEPS):
            following = []
            for depth in range(STEPS - taken):
                across = now[depth + 1] if depth == 0 else now[depth - 1] + now[depth + 1]
                following.append(step(now[depth], across, prev[depth], side[depth], missing[depth]))
            prev, now = now, following
            if taken < STEPS - 1:
                out[taken * rows] = now[0]
            else:
                out[4 * rows] = now[0][:own_rows]
        code = class_ref[place[0]].astype(F32)
        out[3 * rows] = code
        which = 2 * half + (place[0] % half)
        low, high = received(which)
        if place[0] < half:
            halo = jnp.where(lower, high, pltpu.roll(low, TILE // 2, 0))
        else:
            halo = jnp.where(lower, pltpu.roll(high, TILE // 2, 0), low)
        out[3 * rows + own_rows] = halo
        out[4 * rows + own_rows] = class_ref[place[1]].astype(F32)
        sides.append(out)
    for start, left in sides[0].items():
        right = sides[1][start]
        place = pl.ds(start, left.shape[0])
        first_ref[place] = jnp.where(odd_x, right, left)
        second_ref[place] = jnp.where(odd_x, left, right)


def evolve(
    c_ref, e_ref, s_ref, m_ref, ch_ref, eh_ref, sh_ref, mh_ref, g_ref, odd, even
):
    nx, own_rows, _ = c_ref.shape
    rows = own_rows + TILE

    def sweep(read, read_earlier, write):
        planes = [read(x) for x in range(nx)]
        for x in range(nx):
            across = sum(planes[beside] for beside in (x - 1, x + 1) if 0 <= beside < nx)
            side, missing = joined(s_ref, sh_ref, x), joined(m_ref, mh_ref, x)
            write(x, step(planes[x], across, read_earlier(x), side, missing))

    def store(ref):
        def write(x, value):
            ref[x] = value

        return write

    def last(x, value):
        g_ref[x] = value[:own_rows]

    start = lambda x: joined(c_ref, ch_ref, x)
    sweep(start, lambda x: joined(e_ref, eh_ref, x), store(odd))
    sweep(lambda x: odd[x], start, store(even))
    sweep(lambda x: even[x], lambda x: odd[x], store(odd))
    sweep(lambda x: odd[x], lambda x: even[x], last)


def add_neighbours(
    table, got_first, got_second, first_ref, second_ref, s_ref, m_ref, sh_ref, mh_ref, g_ref, out_ref, edges, sems
):
    nx, own_rows, _ = s_ref.shape
    odd = lax.axis_index("gx") % 2 == 1
    rows = own_rows + TILE
    inner = pltpu.make_async_copy(
        g_ref.at[pl.ds(STEPS, nx - 2 * STEPS)], out_ref.at[pl.ds(STEPS, nx - 2 * STEPS)], sems.at[0]
    )
    inner.start()
    copies = [inner]
    zeros = jnp.zeros((TILE, s_ref.shape[2]), F32)
    for end, (edge, inward) in enumerate(((0, 1), (nx - 1, -1))):
        swapped = odd if end == 0 else jnp.logical_not(odd)

        def picked(first, second, start, count):
            place = pl.ds(start, count)
            return jnp.where(swapped, second[place], first[place])

        got = lambda start, count: picked(got_first, got_second, start, count)
        own = lambda start, count: picked(first_ref, second_ref, start, count)
        place = [edge + inward * depth for depth in range(STEPS)]
        w0, w1, w2, w3 = [joined(s_ref, sh_ref, x) for x in place]
        k0, k1, k2 = [joined(m_ref, mh_ref, x) for x in place[:3]]
        fm0, fm1, fm2 = [got(t * rows, rows) for t in range(3)]
        fo0, fo1, fo2 = [own(t * rows, rows) for t in range(3)]
        fm3 = jnp.concatenate([got(4 * rows, own_rows), zeros], axis=0)
        v1, j1, _ = weights(got(3 * rows, rows).astype(jnp.int32), table)
        v2, _, _ = weights(got(4 * rows + own_rows, own_rows).astype(jnp.int32), table)
        v2 = jnp.concatenate([v2, zeros], axis=0)
        a1 = v1 * fo0
        b1 = w0 * fm0
        a2 = v1 * ((lateral(a1) + j1 * a1) + (b1 + fo1))
        z2 = v2 * a1
        b2 = w0 * ((lateral(b1) + k0 * b1) + (a1 + fm1))
        c2 = w1 * b1
        a3 = a1 + v1 * ((lateral(a2) + j1 * a2) + ((z2 + b2) + (fo2 - 6.0 * a1)))
        b3 = b1 + w0 * ((lateral(b2) + k0 * b2) + ((a2 + c2) + (fm2 - 6.0 * b1)))
        c3 = w1 * ((lateral(c2) + k1 * c2) + b2)
        d3 = w2 * c2
        b4 = b2 + w0 * ((lateral(b3) + k0 * b3) + ((a3 + c3) + (fm3 - 6.0 * b2)))
        c4 = c2 + w1 * ((lateral(c3) + k1 * c3) + ((b3 + d3) - 6.0 * c2))
        d4 = w2 * ((lateral(d3) + k2 * d3) + c3)
        e4 = w3 * d3
        first = min(place)
        for x, value in zip(place, (b4, c4, d4, e4)):
            edges[end, x - first] = g_ref[x] + value[:own_rows]
        copy = pltpu.make_async_copy(edges.at[end], out_ref.at[pl.ds(first, STEPS)], sems.at[end + 1])
        copy.start()
        copies.append(copy)
    for copy in copies:
        copy.wait()


def swapped(array, axis, start):
    pairs = [(i, i + 1) for i in range(start, lax.axis_size(axis) - 1, 2)]
    return lax.ppermute(array, axis, pairs + [(j, i) for i, j in pairs])


def vmem(*shape):
    return jax.ShapeDtypeStruct(shape, F32)


def on_device(pressure_now, pressure_prev, node_class, admittance):
    nx, ny, nz = pressure_now.shape
    rows = ny + TILE
    cells = nx * ny * nz
    inputs = [pltpu.with_memory_space_constraint(x, pltpu.HBM) for x in (pressure_now, pressure_prev, node_class)]
    packed = vmem(3 * nx // 2, TILE, nz)
    cross, chip = pl.pallas_call(
        pack_rows,
        out_shape=[packed, packed],
        in_specs=[HBM] * 3,
        out_specs=[VMEM] * 2,
        scratch_shapes=[
            pltpu.VMEM((2, 2, nx, TILE, nz), F32),
            pltpu.VMEM((2, nx, TILE, nz), jnp.int32),
            pltpu.SemaphoreType.DMA((3, 2)),
        ],
        compiler_params=PARAMS,
        cost_estimate=cost(cells, 4 * cells),
        name="pack_rows",
    )(*inputs)
    cross = swapped(cross, "gy", 1)
    chip = swapped(chip, "gy", 0)
    *own, code = pl.pallas_call(
        own_state,
        out_shape=[vmem(nx, ny, nz)] * 4 + [jax.ShapeDtypeStruct((nx, ny, nz), jnp.int32)],
        in_specs=[SMEM] + [HBM] * 3,
        out_specs=[VMEM] * 5,
        scratch_shapes=[pltpu.VMEM((nx, ny, nz), F32)] * 2 + [pltpu.SemaphoreType.DMA((3, CHUNKS))],
        compiler_params=PARAMS,
        cost_estimate=cost(30 * cells, 28 * cells),
        name="own_state",
    )(admittance, *inputs)
    plane = vmem(4 * rows + 2 * ny, nz)
    *halo, first, second = pl.pallas_call(
        pack_planes,
        out_shape=[vmem(nx, TILE, nz)] * 4 + [plane, plane],
        in_specs=[SMEM] + [VMEM] * 7,
        out_specs=[VMEM] * 6,
        compiler_params=PARAMS,
        cost_estimate=cost(10 * cells, 4 * cells),
        name="pack_planes",
    )(admittance, cross, chip, code, *own)
    got_first = swapped(first, "gx", 1)
    got_second = swapped(second, "gx", 0)
    free = pl.pallas_call(
        evolve,
        out_shape=vmem(nx, ny, nz),
        in_specs=[VMEM] * 8,
        out_specs=VMEM,
        scratch_shapes=[pltpu.VMEM((nx, rows, nz), F32)] * 2,
        compiler_params=PARAMS,
        cost_estimate=cost(60 * cells, 40 * cells),
        name="evolve",
    )(*own, *halo)
    return pl.pallas_call(
        add_neighbours,
        out_shape=vmem(nx, ny, nz),
        in_specs=[SMEM] + [VMEM] * 9,
        out_specs=HBM,
        scratch_shapes=[pltpu.VMEM((2, STEPS, ny, nz), F32), pltpu.SemaphoreType.DMA((3,))],
        compiler_params=PARAMS,
        cost_estimate=cost(10 * cells, 4 * cells),
        name="add_neighbours",
    )(admittance, got_first, got_second, first, second, own[2], own[3], halo[2], halo[3], free)


def solution(mesh):
    return jax.shard_map(
        on_device,
        mesh=mesh,
        in_specs=(P("gx", "gy", None), P("gx", "gy", None), P("gx", "gy", None), P()),
        out_specs=P("gx", "gy", None),
        check_vma=False,
    )
```

time: 43 us -> 30.7 us (0.71)
  the two profiles are of different devices: /device:TPU:219 before, /device:TPU:1 now
where the time goes in v2:
time: 30.7 us; the launch traced here: 30.5 us
  starting transfers between devices  15.7 us (51%)
  Pallas kernels  10.9 us (36%)
  waiting for transfers between devices  3.78 us (12%)
    ppermute x4, starting transfers between devices, swapped(): return lax.ppermute(array, axis, pairs + [(j, i) for i, j in pairs])  15.7 us
    ppermute x4, waiting for transfers between devices, swapped(): return lax.ppermute(array, axis, pairs + [(j, i) for i, j in pairs])  3.78 us
    pallas_call x1, Pallas kernels, on_device(): pl.pallas_call(evolve, out_shape=vmem(nx, ny, nz), in_specs=[VMEM] * 8, o...  3.39 us
    pallas_call x1, Pallas kernels, on_device(): pl.pallas_call(own_state, out_shape=[vmem(nx, ny, nz)] * 4 + [jax.ShapeDt...  2.71 us
    pallas_call x1, Pallas kernels, on_device(): pl.pallas_call(add_neighbours, out_shape=vmem(nx, ny, nz), in_specs=[SMEM...  1.86 us
    pallas_call x1, Pallas kernels, on_device(): pl.pallas_call(pack_planes, out_shape=[vmem(nx, TILE, nz)] * 4 + [plane,...  1.52 us
    pallas_call x1, Pallas kernels, on_device(): pl.pallas_call(pack_rows, out_shape=[packed, packed], in_specs=[HBM] * 3,...  1.44 us
  transfers between devices with their start and end apart: 4, of which 1 were waited for; matrix products, arithmetic and copies ran while one was open for 0% of the time, Pallas kernels for 20%

profile of v2, /device:TPU:1, one launch (start us, length us, event | category | flops | bytes accessed | tf_op | source)
XLA Modules:
  0.0 30.5 jit_solution(116388540087140252)
XLA Ops:
  0.0 1.4 %pack_rows.1 = (f32[48,8,256]{2,1,0:T(8,128)S(1)}, f32[48,8,256]{2,1,0:T(8,128)S(1)}) custom-call(f32[32,32,256]{2,1,0:T(8,128)} %now_hbm.1, f32[32,32,256]{2,1,0:T(8,128)} %prev_hbm.1, s32[32,32,256]{2,1,0:T(8,128)} %class_hbm.1), custom_call_target="tpu_custom_call" | custom-call | flops 262144 | bytes 1048576 | tf_op jit(solution)/shard_map/pack_rows/pallas_call | solution.py:301
  1.5 0.0 copy-start
  1.5 4.6 %collective-permute-start = (f32[48,8,256]{2,1,0:T(8,128)S(1)}, f32[48,8,256]{2,1,0:T(8,128)S(1)}, u32[]{:S(2)}, u32[]{:S(2)}) collective-permute-start(f32[48,8,256]{2,1,0:T(8,128)S(1)} %get-tuple-element.18), channel_id=1, source_target_pairs={{1,2},{3,4},{5,6},{7,8},{9,10},{11,12},{13,14},{15,16},{17,18},{19... | collective-permute-start | bytes 1179656 | tf_op jit(solution)/shard_map/ppermute | solution.py:288
  6.1 8.5 %collective-permute-start.1 = (f32[48,8,256]{2,1,0:T(8,128)S(1)}, f32[48,8,256]{2,1,0:T(8,128)S(1)}, u32[]{:S(2)}, u32[]{:S(2)}) collective-permute-start(f32[48,8,256]{2,1,0:T(8,128)S(1)} %get-tuple-element.19), channel_id=1, source_target_pairs={{0,1},{2,3},{4,5},{6,7},{8,9},{10,11},{12,13},{14,15},{16,17},{18,... | collective-permute-start | bytes 1179656 | tf_op jit(solution)/shard_map/ppermute | solution.py:288
  14.6 0.0 copy-done
  14.6 2.7 %own_state.1 = (f32[32,32,256]{2,1,0:T(8,128)S(1)}, f32[32,32,256]{2,1,0:T(8,128)S(1)}, f32[32,32,256]{2,1,0:T(8,128)S(1)}, f32[32,32,256]{2,1,0:T(8,128)S(1)}, s32[32,32,256]{2,1,0:T(8,128)S(1)}) custom-call(f32[8]{0:T(128)S(1)} %copy-done, f32[32,32,256]{2,1,0:T(8,128)} %now_hbm.1, f32[32,32,256]{2,1,0:T(8,128)} %prev_hbm.1, s32[32,32,256]{2,1,0:T(8,128)} %class_hbm.1), custom_call_target="tpu_custom_call" | custom-call | flops 7864320 | bytes 7340032 | tf_op jit(solution)/shard_map/own_state/pallas_call | solution.py:317
  17.3 0.0 collective-permute-done.cross_ref
  17.3 0.0 collective-permute-done.1.chip_ref
  17.3 1.5 %pack_planes.1 = (f32[32,8,256]{2,1,0:T(8,128)S(1)}, f32[32,8,256]{2,1,0:T(8,128)S(1)}, f32[32,8,256]{2,1,0:T(8,128)S(1)}, f32[32,8,256]{2,1,0:T(8,128)S(1)}, f3...) custom-call(f32[8]{0:T(128)S(1)} %copy-done, f32[48,8,256]{2,1,0:T(8,128)S(1)} %collective-permute-done.cross_ref, ...), custom_call_target="tpu_custom_call" | custom-call | flops 2621440 | bytes 1048576 | tf_op jit(solution)/shard_map/pack_planes/pallas_call | solution.py:328
  18.9 0.7 %collective-permute-start.2 = (f32[224,256]{1,0:T(8,128)S(1)}, f32[224,256]{1,0:T(8,128)S(1)}, u32[]{:S(2)}, u32[]{:S(2)}) collective-permute-start(f32[224,256]{1,0:T(8,128)S(1)} %get-tuple-element.25.first_ref), channel_id=1, source_target_pairs={{64,128},{192,256},{320,384},{448,512},{576,640},{128,64},{256,192... | collective-permute-start | bytes 688136 | tf_op jit(solution)/shard_map/ppermute | solution.py:288
  19.5 1.9 %collective-permute-start.3 = (f32[224,256]{1,0:T(8,128)S(1)}, f32[224,256]{1,0:T(8,128)S(1)}, u32[]{:S(2)}, u32[]{:S(2)}) collective-permute-start(f32[224,256]{1,0:T(8,128)S(1)} %get-tuple-element.26.second_ref), channel_id=1, source_target_pairs={{0,64},{128,192},{256,320},{384,448},{512,576},{640,704},{64,0},{1... | collective-permute-start | bytes 688136 | tf_op jit(solution)/shard_map/ppermute | solution.py:288
  21.5 3.4 %evolve.1.g_ref = f32[32,32,256]{2,1,0:T(8,128)S(1)} custom-call(f32[32,32,256]{2,1,0:T(8,128)S(1)} %get-tuple-element.21.c_ref, f32[32,32,256]{2,1,0:T(8,128)S(1)} %get-tuple-element.22.e_ref, f32[32,32,256]{2,1,0:T(8,128)S(1)} %get-tuple-element.23.s_ref, f32[32,32,256]{2,1,0:T(8,128)S(1)} %get-tuple-element.24.m_ref, ...), custom_call_target="tpu_custom_call" | custom-call | flops 15728640 | bytes 10485760 | tf_op jit(solution)/shard_map/evolve/pallas_call | solution.py:339
  24.9 0.0 collective-permute-done.2.got_first
  24.9 3.8 %collective-permute-done.3.got_second = f32[224,256]{1,0:T(8,128)S(1)} collective-permute-done((f32[224,256]{1,0:T(8,128)S(1)}, f32[224,256]{1,0:T(8,128)S(1)}, u32[]{:S(2)}, u32[]{:S(2)}) %collective-permute-start.3) | collective-permute-done | bytes 229408 | tf_op jit(solution)/shard_map/ppermute | solution.py:288
  28.7 1.9 %add_neighbours.1 = f32[32,32,256]{2,1,0:T(8,128)} custom-call(f32[8]{0:T(128)S(1)} %copy-done, f32[224,256]{1,0:T(8,128)S(1)} %collective-permute-done.2.got_first, f32[224,256]{1,0:T(8,128)S(1)} %collective-permute-done.3.got_second, f32[224,256]{1,0:T(8,128)S(1)} %get-tuple-element.25.first_ref, f32[224,256]{1,0:T(8,128)S(1)} %get-tuple-element.26.second_ref, ...), custom_call_target="tpu_custom_call" | custom-call | flops 2621440 | bytes 1048576 | tf_op jit(solution)/shard_map/add_neighbours/pallas_call | solution.py:349
Async XLA Ops:
  1.5 13.1 %copy-start = (f32[8]{0:T(128)S(1)}, f32[8]{0:T(128)}, u32[]{:S(2)}) copy-start(f32[8]{0:T(128)} %table.5) | copy-start | bytes 100
  1.5 15.9 %collective-permute-start = (f32[48,8,256]{2,1,0:T(8,128)S(1)}, f32[48,8,256]{2,1,0:T(8,128)S(1)}, u32[]{:S(2)}, u32[]{:S(2)}) collective-permute-start(f32[48,8,256]{2,1,0:T(8,128)S(1)} %get-tuple-element.18), channel_id=1, source_target_pairs={{1,2},{3,4},{5,6},{7,8},{9,10},{11,12},{13,14},{15,16},{17,18},{19... | collective-permute-start | bytes 1179656 | tf_op jit(solution)/shard_map/ppermute | solution.py:288
  6.1 11.3 %collective-permute-start.1 = (f32[48,8,256]{2,1,0:T(8,128)S(1)}, f32[48,8,256]{2,1,0:T(8,128)S(1)}, u32[]{:S(2)}, u32[]{:S(2)}) collective-permute-start(f32[48,8,256]{2,1,0:T(8,128)S(1)} %get-tuple-element.19), channel_id=1, source_target_pairs={{0,1},{2,3},{4,5},{6,7},{8,9},{10,11},{12,13},{14,15},{16,17},{18,... | collective-permute-start | bytes 1179656 | tf_op jit(solution)/shard_map/ppermute | solution.py:288
  18.9 6.0 %collective-permute-start.2 = (f32[224,256]{1,0:T(8,128)S(1)}, f32[224,256]{1,0:T(8,128)S(1)}, u32[]{:S(2)}, u32[]{:S(2)}) collective-permute-start(f32[224,256]{1,0:T(8,128)S(1)} %get-tuple-element.25.first_ref), channel_id=1, source_target_pairs={{64,128},{192,256},{320,384},{448,512},{576,640},{128,64},{256,192... | collective-permute-start | bytes 688136 | tf_op jit(solution)/shard_map/ppermute | solution.py:288
  19.5 9.1 %collective-permute-start.3 = (f32[224,256]{1,0:T(8,128)S(1)}, f32[224,256]{1,0:T(8,128)S(1)}, u32[]{:S(2)}, u32[]{:S(2)}) collective-permute-start(f32[224,256]{1,0:T(8,128)S(1)} %get-tuple-element.26.second_ref), channel_id=1, source_target_pairs={{0,64},{128,192},{256,320},{384,448},{512,576},{640,704},{64,0},{1... | collective-permute-start | bytes 688136 | tf_op jit(solution)/shard_map/ppermute | solution.py:288

commit v3 on v2

v3 whole, which is shorter than its diff:
```python
import functools

import jax
import jax.numpy as jnp
from jax import lax
from jax.experimental import pallas as pl
from jax.experimental.pallas import tpu as pltpu
from jax.sharding import PartitionSpec as P

STEPS = 4
MATS = 8
TILE = 8
LANES = 128
CHUNKS = 3
UP_FIRST = 2
THIRD = 1.0 / 3.0
ROOT_THIRD = 0.5773502691896258
F32 = jnp.float32
VMEM = pl.BlockSpec(memory_space=pltpu.VMEM)
HBM = pl.BlockSpec(memory_space=pltpu.HBM)
PARAMS = pltpu.CompilerParams(vmem_limit_bytes=40 * 1024 * 1024)


def cost(flops, moved):
    return pl.CostEstimate(flops=flops, bytes_accessed=moved, transcendentals=0)


def weights(code, table):
    bits = [(code & bit) != 0 for bit in (8, 16, 32)]
    level = [table[index : index + 1, :] for index in range(MATS)]
    for bit in bits:
        level = [jnp.where(bit, high, low) for low, high in zip(level[::2], level[1::2])]
    missing = (6 - (code & 7)).astype(F32)
    damping = (ROOT_THIRD * 0.5) * missing * level[0]
    air = code > 0
    side = jnp.where(air, THIRD / (1.0 + damping), 0.0)
    return side, missing, air


def lateral(plane):
    rows, lanes = plane.shape
    tiles = [plane[start : start + TILE] for start in range(0, rows, TILE)]
    row = lax.broadcasted_iota(jnp.int32, tiles[0].shape, 0)
    down = [pltpu.roll(tile, 1, 0) for tile in tiles]
    up = [pltpu.roll(tile, TILE - 1, 0) for tile in tiles]
    along_rows = jnp.concatenate(
        [
            jnp.where(row == 0, down[i - 1], down[i])
            + jnp.where(row == TILE - 1, up[(i + 1) % len(tiles)], up[i])
            for i in range(len(tiles))
        ],
        axis=0,
    )
    parts = [plane[:, start : start + LANES] for start in range(0, lanes, LANES)]
    lane = lax.broadcasted_iota(jnp.int32, parts[0].shape, 1)
    from_below = [0.0] + [pltpu.roll(part, 1, 1) for part in parts]
    from_above = [pltpu.roll(part, LANES - 1, 1) for part in parts] + [0.0]
    along_lanes = jnp.concatenate(
        [
            jnp.where(lane == 0, from_below[i], from_below[i + 1])
            + jnp.where(lane == LANES - 1, from_above[i + 1], from_above[i])
            for i in range(len(parts))
        ],
        axis=1,
    )
    return along_rows + along_lanes


def step(plane, across, earlier, side, missing):
    return earlier + side * ((lateral(plane) + across) + (missing * plane - 6.0 * earlier))


def rolled(tiles, shift):
    return pltpu.roll(tiles, shift % TILE, tiles.ndim - 2)


def pack_rows(
    admittance_ref, now_ref, prev_ref, class_ref,
    cross_ref, chip_ref, table_ref, now_ends, prev_ends, class_ends, edge, code, scalars, sems, end_sems, scalar_sem
):
    odd = lax.axis_index("gy") % 2 == 1
    nx, ny, nz = now_ref.shape
    copies = []
    for which, source in enumerate((now_ref, prev_ref, class_ref)):
        for end, start in enumerate((0, ny - TILE)):
            target = code.at[end] if which == 2 else edge.at[which, end]
            copy = pltpu.make_async_copy(
                source.at[:, pl.ds(start, TILE), :], target, sems.at[which, end]
            )
            copy.start()
            copies.append(copy)
    scalar_copy = pltpu.make_async_copy(admittance_ref, scalars, scalar_sem)
    scalar_copy.start()
    places = [(0, 0, STEPS), (nx - STEPS, STEPS, STEPS)]
    end_copies = fetch((now_ref, prev_ref, class_ref), (now_ends, prev_ends, class_ends), places, end_sems)
    row = lax.broadcasted_iota(jnp.int32, (nx, TILE, nz), 1)
    for copy in copies:
        copy.wait()
    classes = [code[end].astype(F32) for end in range(2)]
    now = [jnp.where(classes[end] > 0.0, edge[0, end], 0.0) for end in range(2)]
    down = jnp.where(row < 4, now[0], jnp.where(row < 7, rolled(edge[1, 0], 4), rolled(classes[0], 7)))
    up = jnp.where(row >= 4, now[1], jnp.where(row >= 1, rolled(edge[1, 1], 4), rolled(classes[1], 1)))
    cross_ref[pl.ds(0, nx)] = jnp.where(odd, up, down)
    chip_ref[pl.ds(0, nx)] = jnp.where(odd, down, up)
    some = nx // 4
    row = row[:some]
    for index in range(4):
        block = [classes[end][index * some : (index + 1) * some] for end in range(2)]
        block = rolled(block[0], 2 * index - 1), rolled(block[1], 2 * index - 5)
        if index == 0:
            down, up = block
        else:
            down = jnp.where(row < 2 * index, down, block[0])
            up = jnp.where(row < 2 * index, up, block[1])
    cross_ref[pl.ds(nx, some)] = jnp.where(odd, up, down)
    chip_ref[pl.ds(nx, some)] = jnp.where(odd, down, up)
    scalar_copy.wait()
    for index in range(MATS):
        table_ref[index : index + 1, :] = jnp.full((1, nz), scalars[index], F32)
    for copies in end_copies:
        for copy in copies:
            copy.wait()


def halo_tile(cross_ref, chip_ref, odd, x, nx):
    some = nx // 4
    index, shelf = x // some, nx + x % some
    row = lax.broadcasted_iota(jnp.int32, cross_ref.shape[1:], 0)
    cross, chip = cross_ref[x], chip_ref[x]
    low, high = jnp.where(odd, chip, cross), jnp.where(odd, cross, chip)
    cross, chip = cross_ref[shelf], chip_ref[shelf]
    low_more, high_more = jnp.where(odd, chip, cross), jnp.where(odd, cross, chip)
    now = jnp.where(row < 4, high, low)
    prev = rolled(jnp.where(row < 4, low, high), 4)
    more = jnp.where(row < 4, rolled(high_more, 1 - 2 * index), rolled(low_more, 5 - 2 * index))
    code = jnp.where(row == 0, rolled(high, 1), jnp.where(row == 7, rolled(low, 7), more))
    return now, prev, code


def put_state(table, place, now, prev, code, c_ref, e_ref, s_ref, m_ref, masked=False):
    side, missing, air = weights(code, table)
    s_ref[place] = side
    m_ref[place] = missing
    c_ref[place] = now if masked else jnp.where(air, now, 0.0)
    e_ref[place] = jnp.where(air, prev, 0.0)


def fetch(sources, targets, places, sems):
    copies = []
    for index, (start, to, count) in enumerate(places):
        copies.append([])
        for which, (source, target) in enumerate(zip(sources, targets)):
            copy = pltpu.make_async_copy(
                source.at[pl.ds(start, count)], target.at[pl.ds(to, count)], sems.at[which, index]
            )
            copy.start()
            copies[-1].append(copy)
    return copies


def joined(own, halo, x):
    return jnp.concatenate([own[x], halo[x]], axis=0)


def pack_planes(
    table, cross_ref, chip_ref, now_ends, prev_ends, class_ends,
    c_ref, e_ref, s_ref, m_ref, ch_ref, eh_ref, sh_ref, mh_ref, first_ref, second_ref, *, nx
):
    odd_y = lax.axis_index("gy") % 2 == 1
    up_first = lax.axis_index("gy") < UP_FIRST
    own_rows = now_ends.shape[1]
    row = lax.broadcasted_iota(jnp.int32, (TILE, c_ref.shape[2]), 0)
    sides = []
    for end in range(2):
        place = [7 - depth if end else depth for depth in range(STEPS)]
        for k in place:
            put_state(table, k, now_ends[k], prev_ends[k], class_ends[k], c_ref, e_ref, s_ref, m_ref)
            now, prev, code = halo_tile(cross_ref, chip_ref, odd_y, k + (nx - 2 * STEPS) * end, nx)
            if k == place[0]:
                class_halo = code
            put_state(table, k, now, prev, code.astype(jnp.int32), ch_ref, eh_ref, sh_ref, mh_ref, True)
        now = [joined(c_ref, ch_ref, k) for k in place]
        prev = [joined(e_ref, eh_ref, k) for k in place[:3]]
        side = [joined(s_ref, sh_ref, k) for k in place[:3]]
        missing = [joined(m_ref, mh_ref, k) for k in place[:3]]
        alone = [now[0]]
        for taken in range(1, STEPS):
            following = []
            for depth in range(STEPS - taken):
                across = now[depth + 1] if depth == 0 else now[depth - 1] + now[depth + 1]
                following.append(step(now[depth], across, prev[depth], side[depth], missing[depth]))
            prev, now = now, following
            alone.append(now[0])
        halos = [values[own_rows:] for values in alone]
        inner = (row == 3) | (row == 4)
        later = jnp.where(row == 3, rolled(halos[2], 3), rolled(halos[2], 5))
        middle = (row >= 2) & (row < 6)
        classes = jnp.where(row < 4, rolled(class_halo, 2), rolled(class_halo, 6))
        sides.append(
            [values[:own_rows] for values in alone]
            + [class_ends[k].astype(F32) for k in place[:2]]
            + [jnp.where(inner, later, halos[0]), jnp.where(middle, classes, halos[1])]
        )
    start = 0
    for left, right in zip(*sides):
        place = pl.ds(start, left.shape[0])
        first_ref[place] = jnp.where(up_first, right, left)
        second_ref[place] = jnp.where(up_first, left, right)
        start += left.shape[0]


def unpacked(read, own_rows):
    parts = [read(index * own_rows, own_rows) for index in range(6)]
    zeroth, first = read(6 * own_rows, TILE), read(6 * own_rows + TILE, TILE)
    row = lax.broadcasted_iota(jnp.int32, zeroth.shape, 0)
    second = jnp.where(row < 4, rolled(zeroth, 5), rolled(zeroth, 3))
    classes = jnp.where(row < 4, rolled(first, 6), rolled(first, 2))
    nothing = jnp.zeros_like(first)
    halos = [zeroth, first, second, nothing, classes, nothing]
    return [jnp.concatenate(pair, axis=0) for pair in zip(parts, halos)]


def evolve(
    table, now_hbm, prev_hbm, class_hbm, cross_ref, chip_ref,
    ce_ref, ee_ref, se_ref, me_ref, ceh_ref, eeh_ref, seh_ref, meh_ref,
    g_ref, odd, even, now, prev, code, c_ref, e_ref, s_ref, m_ref, ch_ref, eh_ref, sh_ref, mh_ref, sems
):
    nx, own_rows, _ = now_hbm.shape
    middle = nx - 2 * STEPS
    chunk = middle // CHUNKS
    places = [(STEPS + index * chunk, index * chunk, chunk) for index in range(CHUNKS)]
    copies = fetch((now_hbm, prev_hbm, class_hbm), (now, prev, code), places, sems)
    odd_y = lax.axis_index("gy") % 2 == 1
    for k in range(middle):
        halo_now, halo_prev, halo_code = halo_tile(cross_ref, chip_ref, odd_y, k + STEPS, nx)
        put_state(table, k, halo_now, halo_prev, halo_code.astype(jnp.int32), ch_ref, eh_ref, sh_ref, mh_ref, True)

    def body(k, carry):
        put_state(table, k, now[k], prev[k], code[k], c_ref, e_ref, s_ref, m_ref)
        return carry

    for index in range(CHUNKS):
        for copy in copies[index]:
            copy.wait()
        lax.fori_loop(index * chunk, (index + 1) * chunk, body, 0, unroll=4)

    def picked(edge, edge_halo, own, halo):
        def read(x):
            if x < STEPS:
                return joined(edge, edge_halo, x)
            if x >= nx - STEPS:
                return joined(edge, edge_halo, x - middle)
            return joined(own, halo, x - STEPS)

        return read

    start = picked(ce_ref, ceh_ref, c_ref, ch_ref)
    before = picked(ee_ref, eeh_ref, e_ref, eh_ref)
    sides = picked(se_ref, seh_ref, s_ref, sh_ref)
    missing = picked(me_ref, meh_ref, m_ref, mh_ref)

    def sweep(read, read_earlier, write):
        planes = [read(x) for x in range(nx)]
        for x in range(nx):
            across = sum(planes[beside] for beside in (x - 1, x + 1) if 0 <= beside < nx)
            write(x, step(planes[x], across, read_earlier(x), sides(x), missing(x)))

    def store(ref):
        def write(x, value):
            ref[x] = value

        return write

    def last(x, value):
        g_ref[x] = value[:own_rows]

    sweep(start, before, store(odd))
    sweep(lambda x: odd[x], start, store(even))
    sweep(lambda x: even[x], lambda x: odd[x], store(odd))
    sweep(lambda x: odd[x], lambda x: even[x], last)


def add_neighbours(
    table, got_first, got_second, first_ref, second_ref, s_ref, m_ref, sh_ref, mh_ref, g_ref, out_ref, edges, sems
):
    nx, own_rows, _ = g_ref.shape
    up_first = lax.axis_index("gy") < UP_FIRST
    chunk = (nx - 2 * STEPS) // CHUNKS
    copies = []
    for index in range(CHUNKS):
        place = pl.ds(STEPS + index * chunk, chunk)
        copies.append(pltpu.make_async_copy(g_ref.at[place], out_ref.at[place], sems.at[index]))
        copies[-1].start()
    for end in range(2):
        up = up_first if end else jnp.logical_not(up_first)

        def picked(yes, no):
            def read(start, count):
                place = pl.ds(start, count)
                return jnp.where(up, yes[place], no[place])

            return read

        fm0, fm1, fm2, fm3, code1, code2 = unpacked(picked(got_second, got_first), own_rows)
        fo0, fo1, fo2, _, _, _ = unpacked(picked(first_ref, second_ref), own_rows)
        place = [7 - depth if end else depth for depth in range(STEPS)]
        w0, w1, w2, w3 = [joined(s_ref, sh_ref, k) for k in place]
        k0, k1, k2 = [joined(m_ref, mh_ref, k) for k in place[:3]]
        v1, j1, _ = weights(code1.astype(jnp.int32), table)
        v2, _, _ = weights(code2.astype(jnp.int32), table)
        a1 = v1 * fo0
        b1 = w0 * fm0
        a2 = v1 * ((lateral(a1) + j1 * a1) + (b1 + fo1))
        z2 = v2 * a1
        b2 = w0 * ((lateral(b1) + k0 * b1) + (a1 + fm1))
        c2 = w1 * b1
        a3 = a1 + v1 * ((lateral(a2) + j1 * a2) + ((z2 + b2) + (fo2 - 6.0 * a1)))
        b3 = b1 + w0 * ((lateral(b2) + k0 * b2) + ((a2 + c2) + (fm2 - 6.0 * b1)))
        c3 = w1 * ((lateral(c2) + k1 * c2) + b2)
        d3 = w2 * c2
        b4 = b2 + w0 * ((lateral(b3) + k0 * b3) + ((a3 + c3) + (fm3 - 6.0 * b2)))
        c4 = c2 + w1 * ((lateral(c3) + k1 * c3) + ((b3 + d3) - 6.0 * c2))
        d4 = w2 * ((lateral(d3) + k2 * d3) + c3)
        e4 = w3 * d3
        for k, value in zip(place, (b4, c4, d4, e4)):
            edges[k] = g_ref[k + (nx - 2 * STEPS) * end] + value[:own_rows]
    for end in range(2):
        copy = pltpu.make_async_copy(
            edges.at[pl.ds(STEPS * end, STEPS)],
            out_ref.at[pl.ds((nx - STEPS) * end, STEPS)],
            sems.at[CHUNKS + end],
        )
        copy.start()
        copies.append(copy)
    for copy in copies:
        copy.wait()


def shifted(array, up_below):
    nx, ny = lax.axis_size("gx"), lax.axis_size("gy")
    pairs = []
    for j in range(ny):
        up = j < up_below if up_below >= 0 else j >= -up_below
        for i in range(nx - 1):
            low, high = i * ny + j, (i + 1) * ny + j
            pairs.append((low, high) if up else (high, low))
    return lax.ppermute(array, ("gx", "gy"), pairs)


def swapped(array, axis, start):
    pairs = [(i, i + 1) for i in range(start, lax.axis_size(axis) - 1, 2)]
    return lax.ppermute(array, axis, pairs + [(j, i) for i, j in pairs])


def vmem(*shape):
    return jax.ShapeDtypeStruct(shape, F32)


def on_device(pressure_now, pressure_prev, node_class, admittance):
    nx, ny, nz = pressure_now.shape
    rows = ny + TILE
    cells = nx * ny * nz
    middle = nx - 2 * STEPS
    inputs = [
        pltpu.with_memory_space_constraint(x, pltpu.HBM)
        for x in (admittance, pressure_now, pressure_prev, node_class)
    ]
    packed = vmem(nx + nx // 4, TILE, nz)
    edge = vmem(2 * STEPS, ny, nz)
    edge_code = jax.ShapeDtypeStruct(edge.shape, jnp.int32)
    cross, chip, table, *ends = pl.pallas_call(
        pack_rows,
        out_shape=[packed, packed, vmem(MATS, nz), edge, edge, edge_code],
        in_specs=[HBM] * 4,
        out_specs=[VMEM] * 6,
        scratch_shapes=[
            pltpu.VMEM((2, 2, nx, TILE, nz), F32),
            pltpu.VMEM((2, nx, TILE, nz), jnp.int32),
            pltpu.SMEM((MATS,), F32),
            pltpu.SemaphoreType.DMA((3, 2)),
            pltpu.SemaphoreType.DMA((3, 2)),
            pltpu.SemaphoreType.DMA,
        ],
        compiler_params=PARAMS,
        cost_estimate=cost(cells, 4 * cells),
        name="pack_rows",
    )(*inputs)
    cross = swapped(cross, "gy", 1)
    chip = swapped(chip, "gy", 0)
    plane = vmem(6 * ny + 2 * TILE, nz)
    packs = pl.pallas_call(
        functools.partial(pack_planes, nx=nx),
        out_shape=[edge] * 4 + [vmem(2 * STEPS, TILE, nz)] * 4 + [plane, plane],
        in_specs=[VMEM] * 6,
        out_specs=[VMEM] * 10,
        compiler_params=PARAMS,
        cost_estimate=cost(10 * cells, 4 * cells),
        name="pack_planes",
    )(table, cross, chip, *ends)
    edges, halos, (first, second) = packs[:4], packs[4:8], packs[8:]
    got_first = shifted(first, UP_FIRST)
    got_second = shifted(second, -UP_FIRST)
    free = pl.pallas_call(
        evolve,
        out_shape=vmem(nx, ny, nz),
        in_specs=[VMEM] + [HBM] * 3 + [VMEM] * 10,
        out_specs=VMEM,
        scratch_shapes=[pltpu.VMEM((nx, rows, nz), F32)] * 2
        + [pltpu.VMEM((middle, ny, nz), F32)] * 2
        + [pltpu.VMEM((middle, ny, nz), jnp.int32)]
        + [pltpu.VMEM((middle, ny, nz), F32)] * 4
        + [pltpu.VMEM((middle, TILE, nz), F32)] * 4
        + [pltpu.SemaphoreType.DMA((3, CHUNKS))],
        compiler_params=PARAMS,
        cost_estimate=cost(60 * cells, 40 * cells),
        name="evolve",
    )(table, *inputs[1:], cross, chip, *edges, *halos)
    return pl.pallas_call(
        add_neighbours,
        out_shape=vmem(nx, ny, nz),
        in_specs=[VMEM] * 10,
        out_specs=HBM,
        scratch_shapes=[pltpu.VMEM(edge.shape, F32), pltpu.SemaphoreType.DMA((CHUNKS + 2,))],
        compiler_params=PARAMS,
        cost_estimate=cost(10 * cells, 4 * cells),
        name="add_neighbours",
    )(table, got_first, got_second, first, second, edges[2], edges[3], halos[2], halos[3], free)


def solution(mesh):
    return jax.shard_map(
        on_device,
        mesh=mesh,
        in_specs=(P("gx", "gy", None), P("gx", "gy", None), P("gx", "gy", None), P()),
        out_specs=P("gx", "gy", None),
        check_vma=False,
    )
```

time: 30.7 us -> 28.3 us (0.922)
  Pallas kernels: 10.9 us -> 9.06 us
  waiting for transfers between devices: 3.78 us -> 3.21 us
    ppermute x4 -> x2, starting transfers between devices: 15.7 us -> 13.1 us  [swapped(): return lax.ppermute(array, axis, pairs + [(j, i) for i, j in pairs])]
    ppermute x0 -> x2, starting transfers between devices: none -> 2.59 us  [shifted(): return lax.ppermute(array, ('gx', 'gy'), pairs)]
    ppermute x4 -> x2, waiting for transfers between devices: 3.78 us -> 1.23 us  [swapped(): return lax.ppermute(array, axis, pairs + [(j, i) for i, j in pairs])]
    ppermute x0 -> x2, waiting for transfers between devices: none -> 1.98 us  [shifted(): return lax.ppermute(array, ('gx', 'gy'), pairs)]
    pallas_call x5 -> x4, Pallas kernels: 10.9 us -> 9.06 us  [the longest x1 5.06 us: on_device(): pl.pallas_call(evolve, out_shape=vmem(nx, ny, nz), in_specs=[VMEM] + [HBM...]
  transfers between devices with their start and end apart: 4 -> 4, of which waited for: 1 -> 2; matrix products, arithmetic and copies ran while one was open for 0% -> 0% of each run, Pallas kernels for 20% -> 18%
where the time goes in v3:
time: 28.3 us; the launch traced here: 28 us
  starting transfers between devices  15.7 us (55%)
  Pallas kernels  9.06 us (32%)
  waiting for transfers between devices  3.21 us (11%)
    ppermute x2, starting transfers between devices, swapped(): return lax.ppermute(array, axis, pairs + [(j, i) for i, j in pairs])  13.1 us
    pallas_call x1, Pallas kernels, on_device(): pl.pallas_call(evolve, out_shape=vmem(nx, ny, nz), in_specs=[VMEM] + [HBM...  5.06 us
    ppermute x2, starting transfers between devices, shifted(): return lax.ppermute(array, ('gx', 'gy'), pairs)  2.59 us
    ppermute x2, waiting for transfers between devices, shifted(): return lax.ppermute(array, ('gx', 'gy'), pairs)  1.98 us
    pallas_call x1, Pallas kernels, on_device(): pl.pallas_call(pack_rows, out_shape=[packed, packed, vmem(MATS, nz), edge...  1.89 us
    pallas_call x1, Pallas kernels, on_device(): pl.pallas_call(add_neighbours, out_shape=vmem(nx, ny, nz), in_specs=[VMEM...  1.46 us
    ppermute x2, waiting for transfers between devices, swapped(): return lax.ppermute(array, axis, pairs + [(j, i) for i, j in pairs])  1.23 us
    pallas_call x1, Pallas kernels, on_device(): pl.pallas_call(functools.partial(pack_planes, nx=nx), out_shape=[edge] *...  0.65 us
  transfers between devices with their start and end apart: 4, of which 2 were waited for; matrix products, arithmetic and copies ran while one was open for 0% of the time, Pallas kernels for 18%

profile of v3, /device:TPU:1, one launch (start us, length us, event | category | flops | bytes accessed | tf_op | source)
XLA Modules:
  0.0 28.0 jit_solution(8061267973797905257)
XLA Ops:
  0.0 1.9 %pack_rows.1 = (f32[40,8,256]{2,1,0:T(8,128)S(1)}, f32[40,8,256]{2,1,0:T(8,128)S(1)}, f32[8,256]{1,0:T(8,128)S(1)}, f32[8,32,256]{2,1,0:T(8,128)S(1)}, f32[8,32,...) custom-call(f32[8]{0:T(128)} %admittance_ref.1, f32[32,32,256]{2,1,0:T(8,128)} %now_hbm.1, f32[32,32,256]{2,1,0:T(8,128)} %prev_hbm.1, ...), custom_call_target="tpu_custom_call" | custom-call | flops 262144 | bytes 1048576 | tf_op jit(solution)/shard_map/pack_rows/pallas_call | solution.py:371
  1.9 4.6 %collective-permute-start = (f32[40,8,256]{2,1,0:T(8,128)S(1)}, f32[40,8,256]{2,1,0:T(8,128)S(1)}, u32[]{:S(2)}, u32[]{:S(2)}) collective-permute-start(f32[40,8,256]{2,1,0:T(8,128)S(1)} %get-tuple-element.22), channel_id=1, source_target_pairs={{1,2},{3,4},{5,6},{7,8},{9,10},{11,12},{13,14},{15,16},{17,18},{19... | collective-permute-start | bytes 983048 | tf_op jit(solution)/shard_map/ppermute | solution.py:352
  6.5 8.5 %collective-permute-start.1 = (f32[40,8,256]{2,1,0:T(8,128)S(1)}, f32[40,8,256]{2,1,0:T(8,128)S(1)}, u32[]{:S(2)}, u32[]{:S(2)}) collective-permute-start(f32[40,8,256]{2,1,0:T(8,128)S(1)} %get-tuple-element.23), channel_id=1, source_target_pairs={{0,1},{2,3},{4,5},{6,7},{8,9},{10,11},{12,13},{14,15},{16,17},{18,... | collective-permute-start | bytes 983048 | tf_op jit(solution)/shard_map/ppermute | solution.py:352
  15.0 0.0 collective-permute-done.cross_ref
  15.0 1.2 %collective-permute-done.1.chip_ref = f32[40,8,256]{2,1,0:T(8,128)S(1)} collective-permute-done((f32[40,8,256]{2,1,0:T(8,128)S(1)}, f32[40,8,256]{2,1,0:T(8,128)S(1)}, u32[]{:S(2)}, u32[]{:S(2)}) %collective-permute-start.1) | collective-permute-done | bytes 327712 | tf_op jit(solution)/shard_map/ppermute | solution.py:352
  16.3 0.6 %pack_planes.1 = (f32[8,32,256]{2,1,0:T(8,128)S(1)}, f32[8,32,256]{2,1,0:T(8,128)S(1)}, f32[8,32,256]{2,1,0:T(8,128)S(1)}, f32[8,32,256]{2,1,0:T(8,128)S(1)}, f3...) custom-call(f32[8,256]{1,0:T(8,128)S(1)} %get-tuple-element.21.table, ...), custom_call_target="tpu_custom_call" | custom-call | flops 2621440 | bytes 1048576 | tf_op jit(solution)/shard_map/pack_planes/pallas_call | solution.py:391
  16.9 1.3 %collective-permute-start.2 = (f32[208,256]{1,0:T(8,128)S(1)}, f32[208,256]{1,0:T(8,128)S(1)}, u32[]{:S(2)}, u32[]{:S(2)}) collective-permute-start(f32[208,256]{1,0:T(8,128)S(1)} %get-tuple-element.27.first_ref), channel_id=1, source_target_pairs={{0,64},{64,128},{128,192},{192,256},{256,320},{320,384},{384,448},... | collective-permute-start | bytes 638984 | tf_op jit(solution)/shard_map/ppermute | solution.py:347
  18.2 1.3 %collective-permute-start.3 = (f32[208,256]{1,0:T(8,128)S(1)}, f32[208,256]{1,0:T(8,128)S(1)}, u32[]{:S(2)}, u32[]{:S(2)}) collective-permute-start(f32[208,256]{1,0:T(8,128)S(1)} %get-tuple-element.28.second_ref), channel_id=1, source_target_pairs={{64,0},{128,64},{192,128},{256,192},{320,256},{384,320},{448,384},... | collective-permute-start | bytes 638984 | tf_op jit(solution)/shard_map/ppermute | solution.py:347
  19.5 5.1 %evolve.1.g_ref = f32[32,32,256]{2,1,0:T(8,128)S(1)} custom-call(f32[8,256]{1,0:T(8,128)S(1)} %get-tuple-element.21.table, f32[32,32,256]{2,1,0:T(8,128)} %now_hbm.1, f32[32,32,256]{2,1,0:T(8,128)} %prev_hbm.1, s32[32,32,256]{2,1,0:T(8,128)} %class_hbm.1, f32[40,8,256]{2,1,0:T(8,128)S(1)} %collective-permute-done.cross_ref, ...), custom_call_target="tpu_custom_call" | custom-call | flops 15728640 | bytes 10485760 | tf_op jit(solution)/shard_map/evolve/pallas_call | solution.py:403
  24.6 0.0 collective-permute-done.2.got_first
  24.6 2.0 %collective-permute-done.3.got_second = f32[208,256]{1,0:T(8,128)S(1)} collective-permute-done((f32[208,256]{1,0:T(8,128)S(1)}, f32[208,256]{1,0:T(8,128)S(1)}, u32[]{:S(2)}, u32[]{:S(2)}) %collective-permute-start.3) | collective-permute-done | bytes 213024 | tf_op jit(solution)/shard_map/ppermute | solution.py:347
  26.6 1.5 %add_neighbours.1 = f32[32,32,256]{2,1,0:T(8,128)} custom-call(f32[8,256]{1,0:T(8,128)S(1)} %get-tuple-element.21.table, f32[208,256]{1,0:T(8,128)S(1)} %collective-permute-done.2.got_first, f32[208,256]{1,0:T(8,128)S(1)} %collective-permute-done.3.got_second, f32[208,256]{1,0:T(8,128)S(1)} %get-tuple-element.27.first_ref, ...), custom_call_target="tpu_custom_call" | custom-call | flops 2621440 | bytes 1048576 | tf_op jit(solution)/shard_map/add_neighbours/pallas_call | solution.py:418
Async XLA Ops:
  1.9 13.1 %collective-permute-start = (f32[40,8,256]{2,1,0:T(8,128)S(1)}, f32[40,8,256]{2,1,0:T(8,128)S(1)}, u32[]{:S(2)}, u32[]{:S(2)}) collective-permute-start(f32[40,8,256]{2,1,0:T(8,128)S(1)} %get-tuple-element.22), channel_id=1, source_target_pairs={{1,2},{3,4},{5,6},{7,8},{9,10},{11,12},{13,14},{15,16},{17,18},{19... | collective-permute-start | bytes 983048 | tf_op jit(solution)/shard_map/ppermute | solution.py:352
  6.5 9.8 %collective-permute-start.1 = (f32[40,8,256]{2,1,0:T(8,128)S(1)}, f32[40,8,256]{2,1,0:T(8,128)S(1)}, u32[]{:S(2)}, u32[]{:S(2)}) collective-permute-start(f32[40,8,256]{2,1,0:T(8,128)S(1)} %get-tuple-element.23), channel_id=1, source_target_pairs={{0,1},{2,3},{4,5},{6,7},{8,9},{10,11},{12,13},{14,15},{16,17},{18,... | collective-permute-start | bytes 983048 | tf_op jit(solution)/shard_map/ppermute | solution.py:352
  16.9 7.7 %collective-permute-start.2 = (f32[208,256]{1,0:T(8,128)S(1)}, f32[208,256]{1,0:T(8,128)S(1)}, u32[]{:S(2)}, u32[]{:S(2)}) collective-permute-start(f32[208,256]{1,0:T(8,128)S(1)} %get-tuple-element.27.first_ref), channel_id=1, source_target_pairs={{0,64},{64,128},{128,192},{192,256},{256,320},{320,384},{384,448},... | collective-permute-start | bytes 638984 | tf_op jit(solution)/shard_map/ppermute | solution.py:347
  18.2 8.4 %collective-permute-start.3 = (f32[208,256]{1,0:T(8,128)S(1)}, f32[208,256]{1,0:T(8,128)S(1)}, u32[]{:S(2)}, u32[]{:S(2)}) collective-permute-start(f32[208,256]{1,0:T(8,128)S(1)} %get-tuple-element.28.second_ref), channel_id=1, source_target_pairs={{64,0},{128,64},{192,128},{256,192},{320,256},{384,320},{448,384},... | collective-permute-start | bytes 638984 | tf_op jit(solution)/shard_map/ppermute | solution.py:347

commit v4 on v3

--- a/solution.py
+++ b/solution.py
@@ -11,8 +11,8 @@
 MATS = 8
 TILE = 8
 LANES = 128
-CHUNKS = 3
-UP_FIRST = 2
+CHUNKS = 4
+PAIRED = 2
 THIRD = 1.0 / 3.0
 ROOT_THIRD = 0.5773502691896258
 F32 = jnp.float32
@@ -74,10 +74,7 @@
     return pltpu.roll(tiles, shift % TILE, tiles.ndim - 2)
 
 
-def pack_rows(
-    admittance_ref, now_ref, prev_ref, class_ref,
-    cross_ref, chip_ref, table_ref, now_ends, prev_ends, class_ends, edge, code, scalars, sems, end_sems, scalar_sem
-):
+def pack_rows(now_ref, prev_ref, class_ref, cross_ref, chip_ref, edge, code, sems):
     odd = lax.axis_index("gy") % 2 == 1
     nx, ny, nz = now_ref.shape
     copies = []
@@ -89,10 +86,6 @@
             )
             copy.start()
             copies.append(copy)
-    scalar_copy = pltpu.make_async_copy(admittance_ref, scalars, scalar_sem)
-    scalar_copy.start()
-    places = [(0, 0, STEPS), (nx - STEPS, STEPS, STEPS)]
-    end_copies = fetch((now_ref, prev_ref, class_ref), (now_ends, prev_ends, class_ends), places, end_sems)
     row = lax.broadcasted_iota(jnp.int32, (nx, TILE, nz), 1)
     for copy in copies:
         copy.wait()
@@ -114,12 +107,6 @@
             up = jnp.where(row < 2 * index, up, block[1])
     cross_ref[pl.ds(nx, some)] = jnp.where(odd, up, down)
     chip_ref[pl.ds(nx, some)] = jnp.where(odd, down, up)
-    scalar_copy.wait()
-    for index in range(MATS):
-        table_ref[index : index + 1, :] = jnp.full((1, nz), scalars[index], F32)
-    for copies in end_copies:
-        for copy in copies:
-            copy.wait()
 
 
 def halo_tile(cross_ref, chip_ref, odd, x, nx):
@@ -158,31 +145,49 @@
     return copies
 
 
-def joined(own, halo, x):
-    return jnp.concatenate([own[x], halo[x]], axis=0)
+def own_state(
+    admittance_ref, now_ref, prev_ref, class_ref,
+    table_ref, c_ref, e_ref, s_ref, m_ref, code, now, prev, scalars, sems, scalar_sem
+):
+    nx, _, nz = now_ref.shape
+    scalar_copy = pltpu.make_async_copy(admittance_ref, scalars, scalar_sem)
+    scalar_copy.start()
+    chunk = nx // CHUNKS
+    places = [(index * chunk, index * chunk, chunk) for index in range(CHUNKS)]
+    copies = fetch((class_ref, now_ref, prev_ref), (code, now, prev), places, sems)
+    scalar_copy.wait()
+    for index in range(MATS):
+        table_ref[index : index + 1, :] = jnp.full((1, nz), scalars[index], F32)
+
+    def body(k, carry):
+        put_state(table_ref, k, now[k], prev[k], code[k], c_ref, e_ref, s_ref, m_ref)
+        return carry
+
+    for index in range(CHUNKS):
+        for copy in copies[index]:
+            copy.wait()
+        lax.fori_loop(index * chunk, (index + 1) * chunk, body, 0, unroll=4)
 
 
 def pack_planes(
-    table, cross_ref, chip_ref, now_ends, prev_ends, class_ends,
-    c_ref, e_ref, s_ref, m_ref, ch_ref, eh_ref, sh_ref, mh_ref, first_ref, second_ref, *, nx
+    table, cross_ref, chip_ref, code_ref, c_ref, e_ref, s_ref, m_ref,
+    ch_ref, eh_ref, sh_ref, mh_ref, first_ref, second_ref
 ):
     odd_y = lax.axis_index("gy") % 2 == 1
-    up_first = lax.axis_index("gy") < UP_FIRST
-    own_rows = now_ends.shape[1]
+    up_first, _ = ways()
+    nx, own_rows, _ = c_ref.shape
     row = lax.broadcasted_iota(jnp.int32, (TILE, c_ref.shape[2]), 0)
     sides = []
     for end in range(2):
         place = [7 - depth if end else depth for depth in range(STEPS)]
-        for k in place:
-            put_state(table, k, now_ends[k], prev_ends[k], class_ends[k], c_ref, e_ref, s_ref, m_ref)
-            now, prev, code = halo_tile(cross_ref, chip_ref, odd_y, k + (nx - 2 * STEPS) * end, nx)
+        planes = [k + (nx - 2 * STEPS) * end for k in place]
+        for k, x in zip(place, planes):
+            now, prev, code = halo_tile(cross_ref, chip_ref, odd_y, x, nx)
             if k == place[0]:
                 class_halo = code
             put_state(table, k, now, prev, code.astype(jnp.int32), ch_ref, eh_ref, sh_ref, mh_ref, True)
-        now = [joined(c_ref, ch_ref, k) for k in place]
-        prev = [joined(e_ref, eh_ref, k) for k in place[:3]]
-        side = [joined(s_ref, sh_ref, k) for k in place[:3]]
-        missing = [joined(m_ref, mh_ref, k) for k in place[:3]]
+        both = lambda own, halo: [jnp.concatenate([own[x], halo[k]], axis=0) for k, x in zip(place, planes)]
+        now, prev, side, missing = both(c_ref, ch_ref), both(e_ref, eh_ref), both(s_ref, sh_ref), both(m_ref, mh_ref)
         alone = [now[0]]
         for taken in range(1, STEPS):
             following = []
@@ -198,7 +203,7 @@
         classes = jnp.where(row < 4, rolled(class_halo, 2), rolled(class_halo, 6))
         sides.append(
             [values[:own_rows] for values in alone]
-            + [class_ends[k].astype(F32) for k in place[:2]]
+            + [code_ref[x].astype(F32) for x in planes[:2]]
             + [jnp.where(inner, later, halos[0]), jnp.where(middle, classes, halos[1])]
         )
     start = 0
@@ -221,43 +226,32 @@
 
 
 def evolve(
-    table, now_hbm, prev_hbm, class_hbm, cross_ref, chip_ref,
-    ce_ref, ee_ref, se_ref, me_ref, ceh_ref, eeh_ref, seh_ref, meh_ref,
-    g_ref, odd, even, now, prev, code, c_ref, e_ref, s_ref, m_ref, ch_ref, eh_ref, sh_ref, mh_ref, sems
+    table, cross_ref, chip_ref, c_ref, e_ref, s_ref, m_ref, ceh_ref, eeh_ref, seh_ref, meh_ref,
+    g_ref, odd, even, ch_ref, eh_ref, sh_ref, mh_ref
 ):
-    nx, own_rows, _ = now_hbm.shape
+    nx, own_rows, _ = c_ref.shape
     middle = nx - 2 * STEPS
-    chunk = middle // CHUNKS
-    places = [(STEPS + index * chunk, index * chunk, chunk) for index in range(CHUNKS)]
-    copies = fetch((now_hbm, prev_hbm, class_hbm), (now, prev, code), places, sems)
     odd_y = lax.axis_index("gy") % 2 == 1
     for k in range(middle):
-        halo_now, halo_prev, halo_code = halo_tile(cross_ref, chip_ref, odd_y, k + STEPS, nx)
-        put_state(table, k, halo_now, halo_prev, halo_code.astype(jnp.int32), ch_ref, eh_ref, sh_ref, mh_ref, True)
-
-    def body(k, carry):
-        put_state(table, k, now[k], prev[k], code[k], c_ref, e_ref, s_ref, m_ref)
-        return carry
-
-    for index in range(CHUNKS):
-        for copy in copies[index]:
-            copy.wait()
-        lax.fori_loop(index * chunk, (index + 1) * chunk, body, 0, unroll=4)
-
-    def picked(edge, edge_halo, own, halo):
+        now, prev, code = halo_tile(cross_ref, chip_ref, odd_y, k + STEPS, nx)
+        put_state(table, k, now, prev, code.astype(jnp.int32), ch_ref, eh_ref, sh_ref, mh_ref, True)
+
+    def picked(own, edge_halo, halo):
         def read(x):
             if x < STEPS:
-                return joined(edge, edge_halo, x)
-            if x >= nx - STEPS:
-                return joined(edge, edge_halo, x - middle)
-            return joined(own, halo, x - STEPS)
+                beyond = edge_halo[x]
+            elif x >= nx - STEPS:
+                beyond = edge_halo[x - middle]
+            else:
+                beyond = halo[x - STEPS]
+            return jnp.concatenate([own[x], beyond], axis=0)
 
         return read
 
-    start = picked(ce_ref, ceh_ref, c_ref, ch_ref)
-    before = picked(ee_ref, eeh_ref, e_ref, eh_ref)
-    sides = picked(se_ref, seh_ref, s_ref, sh_ref)
-    missing = picked(me_ref, meh_ref, m_ref, mh_ref)
+    start = picked(c_ref, ceh_ref, ch_ref)
+    before = picked(e_ref, eeh_ref, eh_ref)
+    sides = picked(s_ref, seh_ref, sh_ref)
+    missing = picked(m_ref, meh_ref, mh_ref)
 
     def sweep(read, read_earlier, write):
         planes = [read(x) for x in range(nx)]
@@ -284,7 +278,7 @@
     table, got_first, got_second, first_ref, second_ref, s_ref, m_ref, sh_ref, mh_ref, g_ref, out_ref, edges, sems
 ):
     nx, own_rows, _ = g_ref.shape
-    up_first = lax.axis_index("gy") < UP_FIRST
+    up_first, right_first = ways()
     chunk = (nx - 2 * STEPS) // CHUNKS
     copies = []
     for index in range(CHUNKS):
@@ -292,20 +286,22 @@
         copies.append(pltpu.make_async_copy(g_ref.at[place], out_ref.at[place], sems.at[index]))
         copies[-1].start()
     for end in range(2):
-        up = up_first if end else jnp.logical_not(up_first)
-
-        def picked(yes, no):
+
+        def picked(is_right, first, second):
+            first, second = (first, second) if end else (second, first)
+
             def read(start, count):
                 place = pl.ds(start, count)
-                return jnp.where(up, yes[place], no[place])
+                return jnp.where(is_right, first[place], second[place])
 
             return read
 
-        fm0, fm1, fm2, fm3, code1, code2 = unpacked(picked(got_second, got_first), own_rows)
-        fo0, fo1, fo2, _, _, _ = unpacked(picked(first_ref, second_ref), own_rows)
+        fm0, fm1, fm2, fm3, code1, code2 = unpacked(picked(right_first, got_first, got_second), own_rows)
+        fo0, fo1, fo2, _, _, _ = unpacked(picked(up_first, first_ref, second_ref), own_rows)
         place = [7 - depth if end else depth for depth in range(STEPS)]
-        w0, w1, w2, w3 = [joined(s_ref, sh_ref, k) for k in place]
-        k0, k1, k2 = [joined(m_ref, mh_ref, k) for k in place[:3]]
+        planes = [k + (nx - 2 * STEPS) * end for k in place]
+        both = lambda own, halo: [jnp.concatenate([own[x], halo[k]], axis=0) for k, x in zip(place, planes)]
+        (w0, w1, w2, w3), (k0, k1, k2, _) = both(s_ref, sh_ref), both(m_ref, mh_ref)
         v1, j1, _ = weights(code1.astype(jnp.int32), table)
         v2, _, _ = weights(code2.astype(jnp.int32), table)
         a1 = v1 * fo0
@@ -336,14 +332,22 @@
         copy.wait()
 
 
-def shifted(array, up_below):
+def ways():
+    row = lax.axis_index("gy")
+    pairs, odd = row < PAIRED, (lax.axis_index("gx") + row) % 2 == 0
+    return pairs & jnp.logical_not(odd), jnp.logical_not(pairs & odd)
+
+
+def moved(array, first):
     nx, ny = lax.axis_size("gx"), lax.axis_size("gy")
     pairs = []
-    for j in range(ny):
-        up = j < up_below if up_below >= 0 else j >= -up_below
-        for i in range(nx - 1):
+    for i in range(nx - 1):
+        for j in range(ny):
             low, high = i * ny + j, (i + 1) * ny + j
-            pairs.append((low, high) if up else (high, low))
+            if j < PAIRED:
+                pairs += [(low, high), (high, low)] if ((i + j) % 2 == 1) == first else []
+            else:
+                pairs.append((high, low) if first else (low, high))
     return lax.ppermute(array, ("gx", "gy"), pairs)
 
 
@@ -366,55 +370,59 @@
         for x in (admittance, pressure_now, pressure_prev, node_class)
     ]
     packed = vmem(nx + nx // 4, TILE, nz)
-    edge = vmem(2 * STEPS, ny, nz)
-    edge_code = jax.ShapeDtypeStruct(edge.shape, jnp.int32)
-    cross, chip, table, *ends = pl.pallas_call(
+    cross, chip = pl.pallas_call(
         pack_rows,
-        out_shape=[packed, packed, vmem(MATS, nz), edge, edge, edge_code],
-        in_specs=[HBM] * 4,
-        out_specs=[VMEM] * 6,
+        out_shape=[packed, packed],
+        in_specs=[HBM] * 3,
+        out_specs=[VMEM] * 2,
         scratch_shapes=[
             pltpu.VMEM((2, 2, nx, TILE, nz), F32),
             pltpu.VMEM((2, nx, TILE, nz), jnp.int32),
-            pltpu.SMEM((MATS,), F32),
             pltpu.SemaphoreType.DMA((3, 2)),
-            pltpu.SemaphoreType.DMA((3, 2)),
-            pltpu.SemaphoreType.DMA,
         ],
         compiler_params=PARAMS,
         cost_estimate=cost(cells, 4 * cells),
         name="pack_rows",
-    )(*inputs)
+    )(*inputs[1:])
     cross = swapped(cross, "gy", 1)
     chip = swapped(chip, "gy", 0)
+    edge = vmem(2 * STEPS, ny, nz)
+    whole = vmem(nx, ny, nz)
+    code = jax.ShapeDtypeStruct(whole.shape, jnp.int32)
+    table, *own, code = pl.pallas_call(
+        own_state,
+        out_shape=[vmem(MATS, nz)] + [whole] * 4 + [code],
+        in_specs=[HBM] * 4,
+        out_specs=[VMEM] * 6,
+        scratch_shapes=[pltpu.VMEM(whole.shape, F32)] * 2
+        + [pltpu.SMEM((MATS,), F32), pltpu.SemaphoreType.DMA((3, CHUNKS)), pltpu.SemaphoreType.DMA],
+        compiler_params=PARAMS,
+        cost_estimate=cost(20 * cells, 4 * cells),
+        name="own_state",
+    )(*inputs)
     plane = vmem(6 * ny + 2 * TILE, nz)
     packs = pl.pallas_call(
-        functools.partial(pack_planes, nx=nx),
-        out_shape=[edge] * 4 + [vmem(2 * STEPS, TILE, nz)] * 4 + [plane, plane],
-        in_specs=[VMEM] * 6,
-        out_specs=[VMEM] * 10,
+        pack_planes,
+        out_shape=[vmem(2 * STEPS, TILE, nz)] * 4 + [plane, plane],
+        in_specs=[VMEM] * 8,
+        out_specs=[VMEM] * 6,
         compiler_params=PARAMS,
         cost_estimate=cost(10 * cells, 4 * cells),
         name="pack_planes",
-    )(table, cross, chip, *ends)
-    edges, halos, (first, second) = packs[:4], packs[4:8], packs[8:]
-    got_first = shifted(first, UP_FIRST)
-    got_second = shifted(second, -UP_FIRST)
+    )(table, cross, chip, code, *own)
+    halos, (first, second) = packs[:4], packs[4:]
+    got_first = moved(first, True)
+    got_second = moved(second, False)
     free = pl.pallas_call(
         evolve,
         out_shape=vmem(nx, ny, nz),
-        in_specs=[VMEM] + [HBM] * 3 + [VMEM] * 10,
+        in_specs=[VMEM] * 11,
         out_specs=VMEM,
-        scratch_shapes=[pltpu.VMEM((nx, rows, nz), F32)] * 2
-        + [pltpu.VMEM((middle, ny, nz), F32)] * 2
-        + [pltpu.VMEM((middle, ny, nz), jnp.int32)]
-        + [pltpu.VMEM((middle, ny, nz), F32)] * 4
-        + [pltpu.VMEM((middle, TILE, nz), F32)] * 4
-        + [pltpu.SemaphoreType.DMA((3, CHUNKS))],
+        scratch_shapes=[pltpu.VMEM((nx, rows, nz), F32)] * 2 + [pltpu.VMEM((middle, TILE, nz), F32)] * 4,
         compiler_params=PARAMS,
         cost_estimate=cost(60 * cells, 40 * cells),
         name="evolve",
-    )(table, *inputs[1:], cross, chip, *edges, *halos)
+    )(table, cross, chip, *own, *halos)
     return pl.pallas_call(
         add_neighbours,
         out_shape=vmem(nx, ny, nz),
@@ -424,7 +432,7 @@
         compiler_params=PARAMS,
         cost_estimate=cost(10 * cells, 4 * cells),
         name="add_neighbours",
-    )(table, got_first, got_second, first, second, edges[2], edges[3], halos[2], halos[3], free)
+    )(table, got_first, got_second, first, second, own[2], own[3], halos[2], halos[3], free)
 
 
 def solution(mesh):

time: 28.3 us -> 27.3 us (0.965)
  waiting for transfers between devices: 3.21 us -> 1.75 us
  Pallas kernels: 9.06 us -> 9.44 us
    ppermute x2, waiting for transfers between devices: 1.23 us -> 0.01 us  [swapped(): return lax.ppermute(array, axis, pairs + [(j, i) for i, j in pairs])]
    pallas_call x3 -> x4, Pallas kernels: 7.6 us -> 7.88 us  [the longest x1 3.63 us: on_device(): pl.pallas_call(evolve, out_shape=vmem(nx, ny, nz), in_specs=[VMEM] * 11,...]
  transfers between devices with their start and end apart: 4 -> 4, of which waited for: 2 -> 1; matrix products, arithmetic and copies ran while one was open for 0% -> 0% of each run, Pallas kernels for 18% -> 22%
where the time goes in v4:
time: 27.3 us; the launch traced here: 27 us
  starting transfers between devices  15.7 us (58%)
  Pallas kernels  9.44 us (35%)
  waiting for transfers between devices  1.75 us (6%)
    ppermute x2, starting transfers between devices, swapped(): return lax.ppermute(array, axis, pairs + [(j, i) for i, j in pairs])  13.1 us
    pallas_call x1, Pallas kernels, on_device(): pl.pallas_call(evolve, out_shape=vmem(nx, ny, nz), in_specs=[VMEM] * 11,...  3.63 us
    ppermute x2, starting transfers between devices, moved(): return lax.ppermute(array, ('gx', 'gy'), pairs)  2.59 us
    pallas_call x1, Pallas kernels, on_device(): pl.pallas_call(own_state, out_shape=[vmem(MATS, nz)] + [whole] * 4 + [cod...  2.19 us
    ppermute x2, waiting for transfers between devices, moved(): return lax.ppermute(array, ('gx', 'gy'), pairs)  1.74 us
    pallas_call x1, Pallas kernels, on_device(): pl.pallas_call(pack_rows, out_shape=[packed, packed], in_specs=[HBM] * 3,...  1.58 us
    pallas_call x1, Pallas kernels, on_device(): pl.pallas_call(add_neighbours, out_shape=vmem(nx, ny, nz), in_specs=[VMEM...  1.56 us
  transfers between devices with their start and end apart: 4, of which 1 were waited for; matrix products, arithmetic and copies ran while one was open for 0% of the time, Pallas kernels for 22%

profile of v4, /device:TPU:1, one launch (start us, length us, event | category | flops | bytes accessed | tf_op | source)
XLA Modules:
  0.0 27.0 jit_solution(573199158827851257)
XLA Ops:
  0.0 1.6 %pack_rows.1 = (f32[40,8,256]{2,1,0:T(8,128)S(1)}, f32[40,8,256]{2,1,0:T(8,128)S(1)}) custom-call(f32[32,32,256]{2,1,0:T(8,128)} %now_ref.3, f32[32,32,256]{2,1,0:T(8,128)} %prev_ref.3, s32[32,32,256]{2,1,0:T(8,128)} %class_ref.3), custom_call_target="tpu_custom_call" | custom-call | flops 262144 | bytes 1048576 | tf_op jit(solution)/shard_map/pack_rows/pallas_call | solution.py:373
  1.6 4.6 %collective-permute-start = (f32[40,8,256]{2,1,0:T(8,128)S(1)}, f32[40,8,256]{2,1,0:T(8,128)S(1)}, u32[]{:S(2)}, u32[]{:S(2)}) collective-permute-start(f32[40,8,256]{2,1,0:T(8,128)S(1)} %get-tuple-element.20), channel_id=1, source_target_pairs={{1,2},{3,4},{5,6},{7,8},{9,10},{11,12},{13,14},{15,16},{17,18},{19... | collective-permute-start | bytes 983048 | tf_op jit(solution)/shard_map/ppermute | solution.py:356
  6.2 8.5 %collective-permute-start.1 = (f32[40,8,256]{2,1,0:T(8,128)S(1)}, f32[40,8,256]{2,1,0:T(8,128)S(1)}, u32[]{:S(2)}, u32[]{:S(2)}) collective-permute-start(f32[40,8,256]{2,1,0:T(8,128)S(1)} %get-tuple-element.21), channel_id=1, source_target_pairs={{0,1},{2,3},{4,5},{6,7},{8,9},{10,11},{12,13},{14,15},{16,17},{18,... | collective-permute-start | bytes 983048 | tf_op jit(solution)/shard_map/ppermute | solution.py:356
  14.7 2.2 %own_state.1 = (f32[8,256]{1,0:T(8,128)S(1)}, f32[32,32,256]{2,1,0:T(8,128)S(1)}, f32[32,32,256]{2,1,0:T(8,128)S(1)}, f32[32,32,256]{2,1,0:T(8,128)S(1)}, f32[32...) custom-call(f32[8]{0:T(128)} %admittance_ref.1, f32[32,32,256]{2,1,0:T(8,128)} %now_ref.3, f32[32,32,256]{2,1,0:T(8,128)} %prev_ref.3, ...), custom_call_target="tpu_custom_call" | custom-call | flops 5242880 | bytes 1048576 | tf_op jit(solution)/shard_map/own_state/pallas_call | solution.py:392
  16.9 0.0 collective-permute-done.cross_ref
  16.9 0.0 collective-permute-done.1.chip_ref
  16.9 0.5 %pack_planes.1 = (f32[8,8,256]{2,1,0:T(8,128)S(1)}, f32[8,8,256]{2,1,0:T(8,128)S(1)}, f32[8,8,256]{2,1,0:T(8,128)S(1)}, f32[8,8,256]{2,1,0:T(8,128)S(1)}, f32[20...) custom-call(f32[8,256]{1,0:T(8,128)S(1)} %get-tuple-element.19.table, f32[40,8,256]{2,1,0:T(8,128)S(1)} %collective-permute-done.cross_ref, ...), custom_call_target="tpu_custom_call" | custom-call | flops 2621440 | bytes 1048576 | tf_op jit(solution)/shard_map/pack_planes/pallas_call | solution.py:404
  17.4 1.9 %collective-permute-start.2 = (f32[208,256]{1,0:T(8,128)S(1)}, f32[208,256]{1,0:T(8,128)S(1)}, u32[]{:S(2)}, u32[]{:S(2)}) collective-permute-start(f32[208,256]{1,0:T(8,128)S(1)} %get-tuple-element.27.first_ref), channel_id=1, source_target_pairs={{1,65},{65,1},{66,2},{67,3},{68,4},{69,5},{70,6},{71,7},{72,8},{73... | collective-permute-start | bytes 638984 | tf_op jit(solution)/shard_map/ppermute | solution.py:351
  19.3 0.7 %collective-permute-start.3 = (f32[208,256]{1,0:T(8,128)S(1)}, f32[208,256]{1,0:T(8,128)S(1)}, u32[]{:S(2)}, u32[]{:S(2)}) collective-permute-start(f32[208,256]{1,0:T(8,128)S(1)} %get-tuple-element.28.second_ref), channel_id=1, source_target_pairs={{0,64},{64,0},{2,66},{3,67},{4,68},{5,69},{6,70},{7,71},{8,72},{9,... | collective-permute-start | bytes 638984 | tf_op jit(solution)/shard_map/ppermute | solution.py:351
  20.0 3.6 %evolve.1.g_ref = f32[32,32,256]{2,1,0:T(8,128)S(1)} custom-call(f32[8,256]{1,0:T(8,128)S(1)} %get-tuple-element.19.table, f32[40,8,256]{2,1,0:T(8,128)S(1)} %collective-permute-done.cross_ref, f32[40,8,256]{2,1,0:T(8,128)S(1)} %collective-permute-done.1.chip_ref, f32[32,32,256]{2,1,0:T(8,128)S(1)} %get-tuple-element.23.c_ref, ...), custom_call_target="tpu_custom_call" | custom-call | flops 15728640 | bytes 10485760 | tf_op jit(solution)/shard_map/evolve/pallas_call | solution.py:416
  23.7 1.7 %collective-permute-done.2.got_first = f32[208,256]{1,0:T(8,128)S(1)} collective-permute-done((f32[208,256]{1,0:T(8,128)S(1)}, f32[208,256]{1,0:T(8,128)S(1)}, u32[]{:S(2)}, u32[]{:S(2)}) %collective-permute-start.2) | collective-permute-done | bytes 213024 | tf_op jit(solution)/shard_map/ppermute | solution.py:351
  25.4 0.0 collective-permute-done.3.got_second
  25.4 1.6 %add_neighbours.1 = f32[32,32,256]{2,1,0:T(8,128)} custom-call(f32[8,256]{1,0:T(8,128)S(1)} %get-tuple-element.19.table, f32[208,256]{1,0:T(8,128)S(1)} %collective-permute-done.2.got_first, f32[208,256]{1,0:T(8,128)S(1)} %collective-permute-done.3.got_second, f32[208,256]{1,0:T(8,128)S(1)} %get-tuple-element.27.first_ref, ...), custom_call_target="tpu_custom_call" | custom-call | flops 2621440 | bytes 1048576 | tf_op jit(solution)/shard_map/add_neighbours/pallas_call | solution.py:426
Async XLA Ops:
  1.6 15.3 %collective-permute-start = (f32[40,8,256]{2,1,0:T(8,128)S(1)}, f32[40,8,256]{2,1,0:T(8,128)S(1)}, u32[]{:S(2)}, u32[]{:S(2)}) collective-permute-start(f32[40,8,256]{2,1,0:T(8,128)S(1)} %get-tuple-element.20), channel_id=1, source_target_pairs={{1,2},{3,4},{5,6},{7,8},{9,10},{11,12},{13,14},{15,16},{17,18},{19... | collective-permute-start | bytes 983048 | tf_op jit(solution)/shard_map/ppermute | solution.py:356
  6.2 10.7 %collective-permute-start.1 = (f32[40,8,256]{2,1,0:T(8,128)S(1)}, f32[40,8,256]{2,1,0:T(8,128)S(1)}, u32[]{:S(2)}, u32[]{:S(2)}) collective-permute-start(f32[40,8,256]{2,1,0:T(8,128)S(1)} %get-tuple-element.21), channel_id=1, source_target_pairs={{0,1},{2,3},{4,5},{6,7},{8,9},{10,11},{12,13},{14,15},{16,17},{18,... | collective-permute-start | bytes 983048 | tf_op jit(solution)/shard_map/ppermute | solution.py:356
  17.4 8.0 %collective-permute-start.2 = (f32[208,256]{1,0:T(8,128)S(1)}, f32[208,256]{1,0:T(8,128)S(1)}, u32[]{:S(2)}, u32[]{:S(2)}) collective-permute-start(f32[208,256]{1,0:T(8,128)S(1)} %get-tuple-element.27.first_ref), channel_id=1, source_target_pairs={{1,65},{65,1},{66,2},{67,3},{68,4},{69,5},{70,6},{71,7},{72,8},{73... | collective-permute-start | bytes 638984 | tf_op jit(solution)/shard_map/ppermute | solution.py:351
  19.3 6.1 %collective-permute-start.3 = (f32[208,256]{1,0:T(8,128)S(1)}, f32[208,256]{1,0:T(8,128)S(1)}, u32[]{:S(2)}, u32[]{:S(2)}) collective-permute-start(f32[208,256]{1,0:T(8,128)S(1)} %get-tuple-element.28.second_ref), channel_id=1, source_target_pairs={{0,64},{64,0},{2,66},{3,67},{4,68},{5,69},{6,70},{7,71},{8,72},{9,... | collective-permute-start | bytes 638984 | tf_op jit(solution)/shard_map/ppermute | solution.py:351
